TPU v7x, 32 devices: a whole 2x2x4 slice. The times are simulated.
32 devices in a mesh: seq: 8 (over z, y), tensor: 4 (over x, core).
Axes of the slice: x: 2, y: 2, z: 4, core: 2. Of those that a mesh axis runs over, the one named last changes fastest.
Arguments:
- hidden: bfloat16 [2048, 2048], P(('seq', 'tensor')), may hold values from -6 to 6
- attn_gain: float32 [2048], replicated, may hold values from 0.25 to 1.75
- attn_query: bfloat16 [2048, 2048], P(None, 'tensor'), may hold values from -0.015625 to 0.015625
- attn_key: bfloat16 [2048, 2048], P(None, 'tensor'), may hold values from -0.125 to 0.125
- attn_value: bfloat16 [2048, 2048], P(None, 'tensor'), may hold values from -0.125 to 0.125
- attn_out: bfloat16 [2048, 2048], P('tensor'), may hold values from -0.125 to 0.125
- ff_gain: float32 [2048], replicated, may hold values from 0.25 to 1.75
- ff_gate: bfloat16 [2048, 5120], P(None, 'tensor'), may hold values from -0.125 to 0.125
- ff_up: bfloat16 [2048, 5120], P(None, 'tensor'), may hold values from -0.125 to 0.125
- ff_down: bfloat16 [5120, 2048], P('tensor'), may hold values from -0.078125 to 0.078125
- final_gain: float32 [2048], replicated, may hold values from 0.25 to 1.75
- embedding: bfloat16 [32128, 2048], P('seq', 'tensor'), may hold values from -0.375 to 0.375
- rel_weight: float32 [32, 32], P(None, 'tensor'), may hold values from -6 to 6
- bucket_table: int32 [2048], replicated, may hold values from 0 to 31
- prefix_kv: bfloat16 [2, 32, 256, 2048], P(None, 'seq', None, 'tensor'), may hold values from -1600 to 1600, as said below
- node_lengths: int32 [32], replicated, may hold values from 1 to 256, 3072 in all
- group_branch: int32 [24], replicated, may hold values from 0 to 6
- node_slot: int32 [32], replicated, may hold values from 0 to 31, each once
- request_group: int32 [8], replicated, may hold values from 0 to 23
Outputs:
- hidden_out: bfloat16 [2048, 2048], P(('seq', 'tensor'))
- last_rms: float32 [8], replicated
- top_logit: float32 [8], replicated
Inputs may be any that keep to these rules, and one draw needn't show every extreme that they name: `prefix_kv`: finite entries.
All inputs are finite; a program needn't handle non-finite values.
Results may differ from a plain program's by a relative error of at most 0.018.
The roundings to bfloat16 on the way count: a program that leaves them out, or rounds other values in their place, can miss the bound.
Values may be sent and summed in bfloat16 or wider, within the bound.
No kernel may reach another device: no remote copies, remote signals or barrier semaphores. Data moves between devices by JAX's collectives and lax.ppermute only.
A program may use at most 192 MiB of HBM per device.

v0:
```python
import jax
import jax.numpy as jnp
from jax import lax
from jax.sharding import PartitionSpec as P

SUF = 256
BRANCHES = 7


def rms_scale(values, gain):
    widened = values.astype(jnp.float32)
    mean_square = jnp.mean(widened * widened, axis=-1, keepdims=True)
    return widened * lax.rsqrt(mean_square + 1e-06) * gain


def shifted_block(bias_slab, query_count, key_span):
    heads_here, slab_len = bias_slab.shape
    tiled = jnp.broadcast_to(bias_slab[:, None, :], (heads_here, query_count, slab_len)).reshape(
        heads_here, query_count * slab_len
    )
    window = lax.slice_in_dim(
        tiled, query_count - 1, query_count - 1 + query_count * (slab_len - 1), axis=1
    )
    return window.reshape(heads_here, query_count, slab_len - 1)[:, :, :key_span]


def attend(queries, key_rows, value_rows, table_bias, query_base, key_start, key_count):
    query_count = queries.shape[0]
    key_span = key_rows.shape[0]
    offset = table_bias.shape[1] // 2
    first_col = offset + key_start - query_base - (query_count - 1)
    bias_slab = lax.dynamic_slice_in_dim(table_bias, first_col, key_span + query_count - 1, 1)
    bias_block = shifted_block(bias_slab, query_count, key_span)
    scores = (
        jnp.einsum("qhe,khe->hqk", queries, key_rows, preferred_element_type=jnp.float32)
        + bias_block
    )
    is_valid = jnp.arange(key_span) < key_count
    scores = jnp.where(is_valid[None, None, :], scores, -1e30)
    row_peak = jnp.max(scores, axis=2)
    weights = jnp.exp(scores - row_peak[:, :, None])
    row_total = jnp.sum(weights, axis=2)
    weighted = jnp.einsum(
        "hqk,khe->qhe", weights.astype(jnp.bfloat16), value_rows, preferred_element_type=jnp.float32
    )
    output = (weighted / jnp.transpose(row_total)[:, :, None]).astype(jnp.bfloat16)
    return (output, jnp.transpose(row_peak), jnp.transpose(row_total))


def combine_parts(outputs, peaks, totals):
    highest = jnp.max(peaks, axis=1, keepdims=True)
    scales = totals * jnp.exp(peaks - highest)
    numer = jnp.sum(scales[..., None] * outputs.astype(jnp.float32), axis=1)
    return numer / jnp.sum(scales, axis=1)[..., None]


def path_info(request_ids, node_lengths, group_branch, request_group):
    group_id = request_group[request_ids]
    branch = 1 + group_branch[group_id]
    group_node = 1 + BRANCHES + group_id
    path_nodes = jnp.stack([jnp.zeros_like(group_id), branch, group_node], axis=1)
    path_counts = node_lengths[path_nodes]
    path_starts = jnp.stack(
        [jnp.zeros_like(branch), path_counts[:, 0], path_counts[:, 0] + path_counts[:, 1]], axis=1
    )
    return (path_nodes, path_starts, jnp.sum(path_counts, axis=1))


def per_device(
    hidden,
    attn_gain,
    attn_query,
    attn_key,
    attn_value,
    attn_out,
    ff_gain,
    ff_gate,
    ff_up,
    ff_down,
    final_gain,
    embedding,
    rel_weight,
    bucket_table,
    prefix_kv,
    node_lengths,
    group_branch,
    node_slot,
    request_group,
):
    n_seq = lax.axis_size("seq")
    n_tensor = lax.axis_size("tensor")
    seq_index = lax.axis_index("seq")
    tensor_index = lax.axis_index("tensor")
    own_rows, width = hidden.shape
    block_rows = own_rows * n_tensor
    heads_here = rel_weight.shape[1]
    head_cols = attn_query.shape[1]
    head_size = head_cols // heads_here
    req_here = block_rows // SUF
    all_requests = req_here * n_seq
    normed = rms_scale(hidden, attn_gain).astype(jnp.bfloat16)
    piece_rows = lax.all_gather(normed, "tensor", axis=0, tiled=True)
    projected = [
        jnp.dot(piece_rows, weight, preferred_element_type=jnp.float32)
        for weight in (attn_query, attn_key, attn_value)
    ]
    projected_rows = jnp.concatenate(projected, axis=1).astype(jnp.bfloat16)
    shaped = (req_here, SUF, heads_here, head_size)
    queries = projected_rows[:, :head_cols]
    key_local = projected_rows[:, head_cols : 2 * head_cols]
    value_local = projected_rows[:, 2 * head_cols :]
    buckets = rel_weight.shape[0]
    one_hot = (bucket_table[:, None] == jnp.arange(buckets)[None, :]).astype(jnp.float32)
    table_bias = jnp.transpose(jnp.dot(one_hot, rel_weight, precision=lax.Precision.HIGHEST))
    request_ids = seq_index * req_here + jnp.arange(req_here)
    path_nodes, path_starts, path_base = path_info(
        request_ids, node_lengths, group_branch, request_group
    )
    query_block = queries.reshape(shaped)
    own_out, own_peak, own_total = jax.vmap(attend, in_axes=(0, 0, 0, None, 0, 0, None))(
        query_block,
        key_local.reshape(shaped),
        value_local.reshape(shaped),
        table_bias,
        path_base,
        path_base,
        SUF,
    )
    cap_rows = prefix_kv.shape[2]
    path_slots = node_slot[path_nodes]
    piece_kv = lax.all_gather(prefix_kv, "seq", axis=1, tiled=True)
    members = piece_kv.shape[1]
    match = (path_slots[:, :, None] == jnp.arange(members)[None, None, :]).astype(jnp.bfloat16)
    placed = jnp.einsum("rlm,smcd->srlcd", match, piece_kv, preferred_element_type=jnp.float32)
    path_kv = placed.astype(jnp.bfloat16)
    level_outs = []
    level_peaks = []
    level_totals = []
    for level in range(3):
        level_keys = path_kv[0, :, level].reshape(req_here, cap_rows, heads_here, head_size)
        level_values = path_kv[1, :, level].reshape(req_here, cap_rows, heads_here, head_size)
        level_count = node_lengths[path_nodes[:, level]]
        output, row_peak, row_total = jax.vmap(attend, in_axes=(0, 0, 0, None, 0, 0, 0))(
            query_block,
            level_keys,
            level_values,
            table_bias,
            path_base,
            path_starts[:, level],
            level_count,
        )
        level_outs.append(output.reshape(block_rows, head_cols))
        level_peaks.append(row_peak.reshape(block_rows, heads_here))
        level_totals.append(row_total.reshape(block_rows, heads_here))
    level_out = jnp.stack(level_outs, axis=1)
    level_peak = jnp.stack(level_peaks, axis=1)
    level_total = jnp.stack(level_totals, axis=1)
    outputs = jnp.concatenate(
        [
            level_out.reshape(block_rows, 3, heads_here, head_size),
            own_out.reshape(block_rows, 1, heads_here, head_size),
        ],
        axis=1,
    )
    peaks = jnp.concatenate([level_peak, own_peak.reshape(block_rows, 1, heads_here)], axis=1)
    totals = jnp.concatenate([level_total, own_total.reshape(block_rows, 1, heads_here)], axis=1)
    attn = combine_parts(outputs, peaks, totals).reshape(block_rows, head_cols).astype(jnp.bfloat16)
    attn_sum = lax.psum_scatter(
        jnp.dot(attn, attn_out, preferred_element_type=jnp.float32),
        "tensor",
        scatter_dimension=0,
        tiled=True,
    )
    mid = (hidden.astype(jnp.float32) + attn_sum).astype(jnp.bfloat16)
    piece_rows = lax.all_gather(
        rms_scale(mid, ff_gain).astype(jnp.bfloat16), "tensor", axis=0, tiled=True
    )
    gate_part = jnp.dot(piece_rows, ff_gate, preferred_element_type=jnp.float32)
    up_part = jnp.dot(piece_rows, ff_up, preferred_element_type=jnp.float32)
    inner = (jax.nn.gelu(gate_part, approximate=True) * up_part).astype(jnp.bfloat16)
    ff_summed = lax.psum_scatter(
        jnp.dot(inner, ff_down, preferred_element_type=jnp.float32).astype(jnp.bfloat16),
        "tensor",
        scatter_dimension=0,
        tiled=True,
    ).astype(jnp.float32)
    hidden_out = (mid.astype(jnp.float32) + ff_summed).astype(jnp.bfloat16)
    offsets = jnp.arange(req_here) * SUF + (SUF - 1) - tensor_index * own_rows
    inside = (offsets >= 0) & (offsets < own_rows)
    picked = hidden_out[jnp.clip(offsets, 0, own_rows - 1)]
    picked = jnp.where(inside[:, None], picked, jnp.zeros((), jnp.bfloat16))
    every_last = lax.all_gather(picked, ("seq", "tensor"), axis=0, tiled=True)
    last_rows = jnp.sum(
        every_last.reshape(n_seq, n_tensor, req_here, width).astype(jnp.float32), axis=1
    ).reshape(all_requests, width)
    mean_square = jnp.mean(last_rows * last_rows, axis=1)
    last_rms = jnp.sqrt(mean_square)
    final_rows = (last_rows * lax.rsqrt(mean_square + 1e-06)[:, None] * final_gain).astype(
        jnp.bfloat16
    )
    embed_cols = embedding.shape[1]
    columns = lax.dynamic_slice_in_dim(final_rows, tensor_index * embed_cols, embed_cols, 1)
    partial_logits = lax.dot_general(
        columns, embedding, (((1,), (1,)), ((), ())), preferred_element_type=jnp.float32
    )
    logits = lax.psum(partial_logits.astype(jnp.bfloat16), "tensor").astype(jnp.float32)
    top_logit = lax.pmax(jnp.max(logits, axis=1), "seq")
    return (hidden_out, last_rms, top_logit)


def solution(mesh):
    return jax.shard_map(
        per_device,
        mesh=mesh,
        in_specs=(
            P(("seq", "tensor"), None),
            P(),
            P(None, "tensor"),
            P(None, "tensor"),
            P(None, "tensor"),
            P("tensor", None),
            P(),
            P(None, "tensor"),
            P(None, "tensor"),
            P("tensor", None),
            P(),
            P("seq", "tensor"),
            P(None, "tensor"),
            P(),
            P(None, "seq", None, "tensor"),
            P(),
            P(),
            P(),
            P(),
        ),
        out_specs=(P(("seq", "tensor"), None), P(), P()),
        check_vma=False,
    )
```

profile of v0, /device:TPU:0, one launch (start us, length us, event | category | flops | bytes accessed | tf_op | source)
XLA Modules:
  0.0 470.2 jit_solution(764327094981056496)
XLA Ops:
  7.2 1.2 fusion.49
  8.5 1.8 fusion.51
  10.4 3.1 copy.77
  17.3 0.7 dynamic-slice.29
  18.7 0.6 gather_fusion.1
  19.4 0.7 reduce_sum.110
  23.8 0.9 fusion.48
  24.8 2.6 broadcast_in_dim.167
  27.4 6.5 %broadcast_in_dim.168 = f32[1,8,130816]{2,1,0:T(8,128)} reshape(f32[8,256,511]{2,1,0:T(8,128)} %broadcast_in_dim.167) | data formatting | bytes 8372224 | tf_op jit(solution)/shard_map/vmap()/broadcast_in_dim | solution.py:18
  33.9 5.4 %slice.176 = f32[1,8,130560]{2,1,0:T(8,128)} slice(f32[1,8,130816]{2,1,0:T(8,128)} %broadcast_in_dim.168), slice={[0:1], [0:8], [255:130815]} | slice | bytes 8355840 | tf_op jit(solution)/shard_map/vmap()/slice | solution.py:21
  39.3 9.0 %reshape.564 = f32[1,8,256,510]{3,2,1,0:T(8,128)} reshape(f32[1,8,130560]{2,1,0:T(8,128)} %slice.176) | data formatting | bytes 8355840 | tf_op jit(solution)/shard_map/vmap()/reshape | solution.py:24
  48.3 3.1 slice.177
  51.5 3.4 copy.104
  54.9 0.6 gather_fusion
  56.9 2.6 broadcast_in_dim.163
  59.5 6.5 %broadcast_in_dim.164 = f32[1,8,130816]{2,1,0:T(8,128)} reshape(f32[8,256,511]{2,1,0:T(8,128)} %broadcast_in_dim.163) | data formatting | bytes 8372224 | tf_op jit(solution)/shard_map/vmap()/broadcast_in_dim | solution.py:18
  66.0 5.4 %slice.173 = f32[1,8,130560]{2,1,0:T(8,128)} slice(f32[1,8,130816]{2,1,0:T(8,128)} %broadcast_in_dim.164), slice={[0:1], [0:8], [255:130815]} | slice | bytes 8355840 | tf_op jit(solution)/shard_map/vmap()/slice | solution.py:21
  71.3 8.3 %reshape.562 = f32[1,8,256,510]{3,2,1,0:T(8,128)} reshape(f32[1,8,130560]{2,1,0:T(8,128)} %slice.173) | data formatting | bytes 8355840 | tf_op jit(solution)/shard_map/vmap()/reshape | solution.py:24
  79.6 3.1 slice.174
  82.8 3.1 copy.103
  87.2 2.6 broadcast_in_dim.157
  89.8 6.5 %broadcast_in_dim.158 = f32[1,8,130816]{2,1,0:T(8,128)} reshape(f32[8,256,511]{2,1,0:T(8,128)} %broadcast_in_dim.157) | data formatting | bytes 8372224 | tf_op jit(solution)/shard_map/vmap()/broadcast_in_dim | solution.py:18
  96.3 5.4 %slice.170 = f32[1,8,130560]{2,1,0:T(8,128)} slice(f32[1,8,130816]{2,1,0:T(8,128)} %broadcast_in_dim.158), slice={[0:1], [0:8], [255:130815]} | slice | bytes 8355840 | tf_op jit(solution)/shard_map/vmap()/slice | solution.py:21
  101.6 8.3 %reshape.560 = f32[1,8,256,510]{3,2,1,0:T(8,128)} reshape(f32[1,8,130560]{2,1,0:T(8,128)} %slice.170) | data formatting | bytes 8355840 | tf_op jit(solution)/shard_map/vmap()/reshape | solution.py:24
  109.9 3.1 slice.171
  113.0 3.2 copy.102
  116.2 2.5 broadcast_in_dim.150
  118.7 7.5 %broadcast_in_dim.151 = f32[1,8,130816]{2,1,0:T(8,128)} reshape(f32[8,256,511]{2,1,0:T(8,128)} %broadcast_in_dim.150) | data formatting | bytes 8372224 | tf_op jit(solution)/shard_map/vmap()/broadcast_in_dim | solution.py:18
  126.2 5.3 %slice.167 = f32[1,8,130560]{2,1,0:T(8,128)} slice(f32[1,8,130816]{2,1,0:T(8,128)} %broadcast_in_dim.151), slice={[0:1], [0:8], [255:130815]} | slice | bytes 8355840 | tf_op jit(solution)/shard_map/vmap()/slice | solution.py:21
  131.5 8.2 %reshape.558 = f32[1,8,256,510]{3,2,1,0:T(8,128)} reshape(f32[1,8,130560]{2,1,0:T(8,128)} %slice.167) | data formatting | bytes 8355840 | tf_op jit(solution)/shard_map/vmap()/reshape | solution.py:24
  139.7 3.0 slice.168
  142.7 3.3 copy.101
  146.0 0.7 fusion.78
  148.6 2.6 convolution_convert_fusion.2
  151.4 2.6 convolution_convert_fusion.4
  154.2 2.6 convolution_convert_fusion.3
  156.9 2.1 fusion.80
  159.4 1.2 fusion.35
  160.5 99.1 %all-gather.7.cloned.1.call-done = bf16[2,32,256,512]{3,2,0,1:T(8,128)(2,1)} async-done(((bf16[2,4,256,512]{3,2,0,1:T(8,128)(2,1)}), bf16[2,32,256,512]{3,2,0,1:T(8,128)(2,1)}) %all-gather.7.cloned.1.call-update) | async-done | bytes 16777232 | tf_op jit(solution)/shard_map/all_gather | solution.py:131
  259.7 15.5 %convert_bitcast_fusion = bf16[2,1,3,256,512]{4,2,3,0,1:T(4,128)(2,1)S(1)} fusion(bf16[2,32,256,512]{3,2,0,1:T(8,128)(2,1)} %all-gather.7.cloned.1.call-done, s32[3]{0:T(128)S(1)} %gather_fusion), kind=kOutput, calls=%fused_computation.21 | convolution fusion | flops 51118176 | bytes 18350092 | tf_op jit(solution)/shard_map/rlm,smcd->srlcd/dot_general | solution.py:134
  275.1 3.4 fusion.77
  278.5 1.9 copy.91
  280.3 1.9 copy.83
  282.2 1.9 copy.89
  284.1 1.9 copy.81
  285.9 1.1 copy.87
  287.5 2.3 fusion.81
  290.1 1.3 copy-done.3
  292.2 1.3 copy-done.4
  297.2 2.1 fusion.84
  299.4 29.7 %reduce-scatter.3.cloned.1.call-done = f32[64,2048]{1,0:T(8,128)} async-done(((f32[256,2048]{1,0:T(8,128)}), f32[64,2048]{1,0:T(8,128)}) %reduce-scatter.3.cloned.1.call-update) | async-done | bytes 524304 | tf_op jit(solution)/shard_map/reduce_scatter | solution.py:168
  329.1 1.2 fusion.53
  330.4 0.8 fusion.55
  331.3 16.8 %all-gather.9.cloned.1.call-done = bf16[256,2048]{1,0:T(8,128)(2,1)} async-done(((bf16[64,2048]{1,0:T(8,128)(2,1)}), bf16[256,2048]{1,0:T(8,128)(2,1)}) %all-gather.9.cloned.1.call-update) | async-done | bytes 1048592 | tf_op jit(solution)/shard_map/all_gather | solution.py:175
  348.1 5.5 %fusion.85 = f32[256,1280]{1,0:T(8,128)} fusion(bf16[256,2048]{1,0:T(8,128)(2,1)} %all-gather.9.cloned.1.call-done, bf16[2048,1280]{1,0:T(8,128)(2,1)} %param.26), kind=kOutput, calls=%fused_computation.130 | convolution fusion | flops 1342177280 | bytes 7602176 | tf_op jit(solution)/shard_map/dot_general | solution.py:178
  353.6 8.7 %convolution_convert_fusion.1 = bf16[256,2048]{1,0:T(8,128)(2,1)} fusion(bf16[1280,2048]{1,0:T(8,128)(2,1)} %param.28, bf16[256,2048]{1,0:T(8,128)(2,1)S(1)} %copy-done.13, bf16[2048,1280]{1,0:T(8,128)(2,1)} %param.27, f32[256,1280]{1,0:T(8,128)} %fusion.85), kind=kOutput, calls=%fused_computation.7 | convolution fusion | flops 2688155648 | bytes 13893632 | tf_op jit(solution)/shard_map/dot_general | solution.py:182
  362.4 0.8 dynamic-slice.40
  363.1 24.3 %reduce-scatter.5.cloned.1.call-done = bf16[64,2048]{1,0:T(8,128)(2,1)} async-done(((bf16[256,2048]{1,0:T(8,128)(2,1)}), bf16[64,2048]{1,0:T(8,128)(2,1)}) %reduce-scatter.5.cloned.1.call-update) | async-done | bytes 262160 | tf_op jit(solution)/shard_map/reduce_scatter | solution.py:181
  387.4 1.0 fusion.56
  388.5 41.3 %all-gather = bf16[32,1,2048]{2,1,0:T(2,128)(2,1)S(1)} all-gather(bf16[1,1,2048]{2,1,0:T(2,128)(2,1)S(1)} %fusion.61), channel_id=1, replica_groups=mesh['seq'=8,'tensor'=4] {'seq','tensor'}, dimensions={0}, use_global_device_ids=true | all-gather | bytes 135168 | tf_op jit(solution)/shard_map/all_gather | solution.py:192
  429.8 0.7 convert_reduce_fusion
  431.4 3.3 convolution_convert_fusion
  434.7 11.0 %psum.7 = bf16[8,4016]{1,0:T(8,128)(2,1)S(1)} all-reduce(bf16[8,4016]{1,0:T(8,128)(2,1)S(1)} %convolution_convert_fusion), channel_id=1, replica_groups=mesh['seq'=8,'tensor'=4] {'tensor'}, use_global_device_ids=true, to_apply=%region_17.18 | all-reduce | flops 32128 | bytes 128512 | tf_op jit(solution)/shard_map/psum | solution.py:206
  445.9 17.6 %pmax.7 = f32[8]{0:T(128)} all-reduce(bf16[8]{0:T(256)(128)(2,1)S(1)} %reduce_max.97), channel_id=1, replica_groups=mesh['seq'=8,'tensor'=4] {'seq'}, use_global_device_ids=true, to_apply=%region_19.20 | all-reduce | flops 8 | bytes 48 | tf_op jit(solution)/shard_map/pmax | solution.py:207
  (80 shorter events, 11.2 us)
Async XLA Ops:
  7.2 290.1 %copy-start = (bf16[512,2048]{1,0:T(8,128)(2,1)S(1)}, bf16[512,2048]{1,0:T(8,128)(2,1)}, u32[]{:S(2)}) copy-start(bf16[512,2048]{1,0:T(8,128)(2,1)} %param.24) | copy-start | bytes 6291460
  7.2 141.4 %all-gather.5.cloned.1.call-start = ((), (), s32[]{:S(2)}) async-start(), calls=%async_computation.2 | async-start | bytes 1310720 | tf_op jit(solution)/shard_map/all_gather | solution.py:102
  10.3 249.4 %all-gather.7.cloned.1.call-start = ((), (), s32[]{:S(2)}) async-start(), calls=%async_computation.3 | async-start | bytes 18874368 | tf_op jit(solution)/shard_map/all_gather | solution.py:131
  13.4 0.7 copy-start.16
  13.4 3.8 copy-start.17
  13.4 5.3 %copy-start.1 = (s32[32]{0:T(128)S(1)}, s32[32]{0:T(128)}, u32[]{:S(2)}) copy-start(s32[32]{0:T(128)} %param.34) | copy-start | bytes 388
  13.4 10.4 %copy-start.14 = (s32[2048]{0:T(1024)S(1)}, s32[2048]{0:T(1024)}, u32[]{:S(2)}) copy-start(s32[2048]{0:T(1024)} %param.32) | copy-start | bytes 24580
  13.4 10.4 %copy-start.15 = (f32[32,8]{0,1:T(8,128)S(1)}, f32[32,8]{0,1:T(8,128)}, u32[]{:S(2)}) copy-start(f32[32,8]{0,1:T(8,128)} %param.31) | copy-start | bytes 3076
  13.5 315.6 %reduce-scatter.3.cloned.1.call-start = ((), (), s32[]{:S(2)}) async-start(), calls=%async_computation.4 | async-start | bytes 2621440 | tf_op jit(solution)/shard_map/reduce_scatter | solution.py:168
  51.4 3.4 copy-start.2
  287.5 2.6 copy-start.6
  289.8 1.6 copy-start.3
  291.9 1.6 copy-start.4
  294.1 1.0 copy-start.9
  294.4 1.1 copy-start.10
  295.5 1.0 copy-start.11
  296.0 1.0 copy-start.8
  299.3 29.8 %copy-start.5 = (bf16[64,2048]{1,0:T(8,128)(2,1)S(1)}, bf16[64,2048]{1,0:T(8,128)(2,1)}, u32[]{:S(2)}) copy-start(bf16[64,2048]{1,0:T(8,128)(2,1)} %param.19) | copy-start | bytes 786436
  299.3 31.0 %copy-start.12 = (f32[2048]{0:T(1024)S(1)}, f32[2048]{0:T(1024)}, u32[]{:S(2)}) copy-start(f32[2048]{0:T(1024)} %param.25) | copy-start | bytes 24580
  299.3 48.7 %all-gather.9.cloned.1.call-start = ((), (), s32[]{:S(2)}) async-start(), calls=%async_computation.5 | async-start | bytes 1310720 | tf_op jit(solution)/shard_map/all_gather | solution.py:175
  331.2 56.2 %reduce-scatter.5.cloned.1.call-start = ((), (), s32[]{:S(2)}) async-start(), calls=%async_computation.6 | async-start | bytes 1310720 | tf_op jit(solution)/shard_map/reduce_scatter | solution.py:181
  348.1 5.5 %copy-start.13 = (bf16[256,2048]{1,0:T(8,128)(2,1)S(1)}, bf16[256,2048]{1,0:T(8,128)(2,1)}, u32[]{:S(2)}) copy-start(bf16[256,2048]{1,0:T(8,128)(2,1)} %all-gather.9.cloned.1.call-done) | copy-start | bytes 3145732
  388.4 46.3 %copy-start.7 = (bf16[64,2048]{1,0:T(8,128)(2,1)}, bf16[64,2048]{1,0:T(8,128)(2,1)S(1)}, u32[]{:S(2)}) copy-start(bf16[64,2048]{1,0:T(8,128)(2,1)S(1)} %fusion.56) | copy-start | bytes 786436
Sparse Core Ops, SparseCore 0:
  10.4 19.4 all-gather.4
  32.0 227.6 all-gather.6
  299.5 29.5 reduce-scatter.2
  331.3 16.7 all-gather.8
  362.5 24.8 reduce-scatter.4
where the time goes:
time: 478 us; the launch traced here: 470 us
  waiting for transfers between devices  170 us (36%)
  local copies, waits for them, and re-layouts  143 us (30%)
  blocking collectives  69.9 us (15%)
  matrix products  51.9 us (11%)
  between operations  23.5 us (5%)
  other arithmetic  11.9 us (2%)
    all_gather x1, waiting for transfers between devices, per_device(): piece_kv = lax.all_gather(prefix_kv, 'seq', axis=1, tiled=True)  99.1 us
    all_gather x1, blocking collectives, per_device(): every_last = lax.all_gather(picked, ('seq', 'tensor'), axis=0, tiled=True)  41.3 us
    broadcast_in_dim x8, local copies, waits for them, and re-layouts, shifted_block(): jnp.broadcast_to(bias_slab[:, None, :], (heads_here, query_count, slab_len))  37.3 us
    reshape x4, local copies, waits for them, and re-layouts, shifted_block(): window.reshape(heads_here, query_count, slab_len - 1)[:, :, :key_span]  33.8 us
    reduce_scatter x1, waiting for transfers between devices, per_device(): lax.psum_scatter(jnp.dot(attn, attn_out, preferred_element_type=jnp.float...  29.7 us
    reduce_scatter x1, waiting for transfers between devices, per_device(): lax.psum_scatter(jnp.dot(inner, ff_down, preferred_element_type=jnp.float...  24.3 us
    slice x4, local copies, waits for them, and re-layouts, shifted_block(): lax.slice_in_dim(tiled, query_count - 1, query_count - 1 + query_count *...  21.4 us
    unnamed x42, local copies, waits for them, and re-layouts  20.3 us
  transfers between devices with their start and end apart: 5, of which 4 were waited for; matrix products, arithmetic and copies ran while one was open for 30% of the time, Pallas kernels for 0%

commit v1 on v0

v1 whole, which is shorter than its diff:
```python
import functools

import jax
import jax.numpy as jnp
from jax import lax
from jax.experimental import pallas as pl
from jax.experimental.pallas import tpu as pltpu
from jax.sharding import PartitionSpec as P

BRANCHES = 7
HEAD = 64
GRAIN = 16
STAGES = 4
MIB = 1 << 20
CLASSES = (
    (256, 224, 160, 64),
    (288, 272, 256, 128),
    (352, 320, 272, 256),
    (448, 384, 320, 272),
    (576, 512, 400, 352),
)


def rms_scale(values, gain):
    widened = values.astype(jnp.float32)
    mean_square = jnp.mean(widened * widened, axis=-1, keepdims=True)
    return widened * lax.rsqrt(mean_square + 1e-06) * gain


def xor_pairs(size, mask):
    return [(i, i ^ mask) for i in range(size)]


def ring_place(index, size):
    half = lax.shift_right_logical(index, jnp.int32(1))
    return jnp.where(lax.bitwise_and(index, jnp.int32(1)) == 0, half, size - 1 - half)


def ring_pairs(size, step):
    order = list(range(0, size, 2)) + list(range(1, size, 2))[::-1]
    return [(order[i], order[(i + step) % size]) for i in range(size)]


def block_order(size):
    bits = size.bit_length() - 1
    return sorted(range(size), key=lambda i: -int(format(i, "b").zfill(bits)[::-1], 2))


def iota(shape, axis):
    return lax.broadcasted_iota(jnp.int32, shape, axis)


def plan_kernel(n_seq, slots_here, cap, classes, lengths, slots, branch_of, groups, table):
    nodes = lengths.shape[1]
    requests = groups.shape[1]
    hop_group = -(-(n_seq // 2) // STAGES)
    eye = iota((nodes, nodes), 0) == iota((nodes, nodes), 1)

    def column(row):
        return jnp.sum(jnp.where(eye, row, 0), axis=1, keepdims=True)

    length = lengths[...]
    slot = slots[...]
    owner = jnp.zeros_like(slot)
    for k in range(1, n_seq):
        owner = owner + (slot >= k * slots_here).astype(jnp.int32)
    inner_slot = slot - owner * slots_here
    place = ring_place(owner, n_seq)
    req_eye = iota((requests, requests), 0) == iota((requests, requests), 1)
    group = jnp.sum(jnp.where(req_eye, groups[...], 0), axis=1, keepdims=True)
    n_groups = branch_of.shape[1]
    branch = jnp.sum(
        jnp.where(iota((requests, n_groups), 1) == group, branch_of[...], 0), axis=1, keepdims=True
    )
    node = iota((requests, nodes), 1)
    need = (node == 0) | (node == 1 + branch) | (node == 1 + BRANCHES + group)
    seats = ring_place(iota((requests, nodes), 0), n_seq)
    ahead = seats - place
    ahead = jnp.where(ahead < 0, ahead + n_seq, ahead)
    best = jnp.full((1, nodes), 1 << 20, jnp.int32)
    forth = jnp.zeros((1, nodes), jnp.int32)
    back = jnp.zeros((1, nodes), jnp.int32)
    for cut in range(n_seq):
        a = jnp.max(jnp.where(need & (ahead <= cut), ahead, 0), axis=0, keepdims=True)
        b = jnp.max(jnp.where(need & (ahead > cut), n_seq - ahead, 0), axis=0, keepdims=True)
        key = jnp.maximum(a, b) * 128 + a + b
        better = key < best
        best = jnp.where(better, key, best)
        forth = jnp.where(better, a, forth)
        back = jnp.where(better, b, back)
    grains = lax.shift_right_logical(length + (GRAIN - 1), jnp.int32(4))
    grains_col = column(grains)
    place_col = column(place)
    earlier = iota((nodes, nodes), 0) < iota((nodes, nodes), 1)
    mine = iota((n_seq, nodes), 0) == place
    offsets = []
    stages = []
    needs = [jnp.zeros((1, 1), jnp.int32)] * STAGES
    for hops in (forth, back):
        stage = jnp.zeros_like(hops)
        for j in range(STAGES):
            stage = stage + (hops > j * hop_group).astype(jnp.int32)
        stage_col = column(stage)
        ahead_of = (stage_col > stage) | ((stage_col == stage) & earlier)
        counted = (place_col == place) & (stage_col > 0) & ahead_of
        offsets.append(jnp.sum(jnp.where(counted, grains_col, 0), axis=0, keepdims=True))
        stages.append(stage)
        for j in range(STAGES):
            rows = jnp.sum(jnp.where(mine & (stage > j), grains, 0), axis=1, keepdims=True)
            needs[j] = jnp.maximum(needs[j], jnp.max(rows, axis=0, keepdims=True))
    choice = jnp.full((1, 1), len(classes) - 1, jnp.int32)
    for number in range(len(classes) - 2, -1, -1):
        fits = needs[0] * GRAIN <= classes[number][0]
        for j in range(1, STAGES):
            fits = fits & (needs[j] * GRAIN <= classes[number][j])
        choice = jnp.where(fits, number, choice)
    table[...] = jnp.zeros_like(table)
    rows = [length, place, forth, back, offsets[0], offsets[1], inner_slot]
    for number, row in enumerate(rows):
        table[number : number + 1, :nodes] = row
    table[7:8, :] = jnp.broadcast_to(choice, (1, table.shape[1]))


def spans(caps):
    edges = [0] + [caps[j] // GRAIN for j in range(STAGES - 1, -1, -1)]
    return [
        (edges[i], edges[i + 1], STAGES - i) for i in range(STAGES) if edges[i + 1] > edges[i]
    ]


def pack_kernel(n_seq, nodes, parts, table, cache, *outs):
    here = ring_place(lax.axis_index("seq"), n_seq)
    width = cache.shape[3]

    def one_node(n, carry):
        @pl.when(table[1, n] == here)
        def _():
            slot = table[6, n]
            count = lax.shift_right_logical(table[0, n] + (GRAIN - 1), 4)
            for way in range(2):
                reach = table[2 + way, n]
                first = table[4 + way, n]
                for number, (low, high, _) in enumerate(parts):
                    target = outs[way * len(parts) + number]
                    start = jnp.maximum(low - first, 0)
                    stop = jnp.where(reach > 0, jnp.minimum(high - first, count), 0)

                    def one_grain(i, inner, target=target, first=first, low=low):
                        source = pl.ds(pl.multiple_of(i * GRAIN, GRAIN), GRAIN)
                        place = pl.ds(pl.multiple_of((first + i - low) * GRAIN, GRAIN), GRAIN)
                        target[place, :width] = cache[0, slot, source, :]
                        target[place, width:] = cache[1, slot, source, :]
                        return inner

                    lax.fori_loop(start, stop, one_grain, 0)

        return carry

    lax.fori_loop(0, nodes, one_node, 0)


def attention_kernel(
    n_seq, n_tensor, order, parts, hop_group, table, groups, branch_of, buckets, weights, proj, cache, *rest
):
    n_landed = len(rest) - 4
    landed, out, own, kept, bias = rest[:n_landed], *rest[n_landed:]
    seq_index = lax.axis_index("seq")
    tensor_index = lax.axis_index("tensor")
    here = ring_place(seq_index, n_seq)
    rows, width = out.shape
    heads = width // HEAD
    cap = cache.shape[2]
    block = rows // n_tensor
    for number, which in enumerate(order):
        seat = lax.bitwise_xor(tensor_index, jnp.int32(which))
        own[pl.ds(pl.multiple_of(seat * block, block), block), :] = proj[
            number * block : (number + 1) * block, :
        ]
    kept[...] = jnp.zeros_like(kept)
    group = groups[0, seq_index]
    path = [jnp.int32(0), 1 + branch_of[0, group], 1 + BRANCHES + group]
    counts = [table[0, n] for n in path]
    starts = [jnp.int32(0), counts[0], counts[0] + counts[1]]
    base = counts[0] + counts[1] + counts[2]
    for level, n in enumerate(path):
        count = lax.shift_right_logical(counts[level] + (GRAIN - 1), 4)
        ahead = here - table[1, n]
        ahead = jnp.where(ahead < 0, ahead + n_seq, ahead)
        local = ahead == 0
        slot = table[6, n]
        forward = ahead <= table[2, n]

        def from_cache(i, inner, level=level, slot=slot):
            place = pl.ds(pl.multiple_of(i * GRAIN, GRAIN), GRAIN)
            kept[level, place, :width] = cache[0, slot, place, :]
            kept[level, place, width:] = cache[1, slot, place, :]
            return inner

        lax.fori_loop(0, jnp.where(local, count, 0), from_cache, 0)
        number = 0
        for way in range(2):
            hop = ahead if way == 0 else n_seq - ahead
            this_way = (~local) & (forward if way == 0 else ~forward)
            first = table[4 + way, n]
            for low, high, stage in parts:
                for step in range(1, stage * hop_group + 1):
                    source = landed[number]
                    number += 1
                    here_it_is = this_way & (hop == step)
                    start = jnp.maximum(low - first, 0)
                    stop = jnp.where(here_it_is, jnp.minimum(high - first, count), 0)

                    def from_ring(i, inner, source=source, low=low, first=first, level=level):
                        place = pl.ds(pl.multiple_of(i * GRAIN, GRAIN), GRAIN)
                        taken = pl.ds(pl.multiple_of((first + i - low) * GRAIN, GRAIN), GRAIN)
                        kept[level, place, :] = source[taken, :]
                        return inner

                    lax.fori_loop(start, stop, from_ring, 0)
    rels = buckets.shape[1]
    bucket = jnp.broadcast_to(buckets[...], (heads, rels))
    reversed_bias = jnp.zeros((heads, rels), jnp.float32)
    for b in range(weights.shape[1]):
        reversed_bias = jnp.where(bucket == b, weights[:, b : b + 1], reversed_bias)
    half = rels // 2
    window = 2 * rows
    for part in range(4):
        shift = (starts[part] - base) if part < 3 else jnp.int32(0)
        turn = half + 1 + shift
        turned = pltpu.roll(reversed_bias, lax.rem(turn + rels, rels), 1)
        bias[part] = jnp.concatenate([turned[:, :rows], turned[:, rels - rows :]], axis=1)
    key_row = iota((cap, 2 * rows), 0)
    half_row = iota((2 * HEAD, rows), 0) < HEAD
    for pair in range(heads // 2):
        cols = slice(pair * 2 * HEAD, (pair + 1) * 2 * HEAD)
        query = jnp.transpose(own[:, cols].astype(jnp.float32))
        query = jnp.concatenate(
            [jnp.where(half_row, query, 0.0), jnp.where(half_row, 0.0, query)], axis=1
        ).astype(jnp.bfloat16)
        scores = []
        for part in range(4):
            if part < 3:
                keys = kept[part, :, cols]
            else:
                keys = own[:, width + pair * 2 * HEAD : width + (pair + 1) * 2 * HEAD]
            score = jnp.dot(keys, query, preferred_element_type=jnp.float32)
            slabs = []
            for head in (2 * pair, 2 * pair + 1):
                line = jnp.broadcast_to(bias[part, head : head + 1, :], (rows // 2, window))
                rolled = pltpu.roll(line, 0, 1, stride=1, stride_axis=0)
                slabs.append(
                    jnp.concatenate(
                        [
                            rolled[:, :rows],
                            jnp.concatenate(
                                [rolled[:, window - rows // 2 :], rolled[:, : rows // 2]], axis=1
                            ),
                        ],
                        axis=0,
                    )
                )
            score = score + jnp.concatenate(slabs, axis=1)
            if part < 3:
                score = jnp.where(key_row < counts[part], score, -1e30)
            scores.append(score)
        peak = jnp.max(scores[0], axis=0, keepdims=True)
        for score in scores[1:]:
            peak = jnp.maximum(peak, jnp.max(score, axis=0, keepdims=True))
        total = jnp.zeros_like(peak)
        summed = jnp.zeros((2 * HEAD, 2 * rows), jnp.float32)
        for part in range(4):
            chance = jnp.exp(scores[part] - peak)
            total = total + jnp.sum(chance, axis=0, keepdims=True)
            if part < 3:
                values = kept[part, :, width + pair * 2 * HEAD : width + (pair + 1) * 2 * HEAD]
            else:
                values = own[:, 2 * width + pair * 2 * HEAD : 2 * width + (pair + 1) * 2 * HEAD]
            summed = summed + lax.dot_general(
                values,
                chance.astype(jnp.bfloat16),
                (((0,), (0,)), ((), ())),
                preferred_element_type=jnp.float32,
            )
        scaled = summed / total
        both = jnp.concatenate([scaled[:HEAD, :rows], scaled[HEAD:, rows:]], axis=0)
        result = jnp.transpose(both).astype(jnp.bfloat16)
        own[:, cols] = result
    for number, which in enumerate(order):
        seat = lax.bitwise_xor(tensor_index, jnp.int32(which))
        out[number * block : (number + 1) * block, :] = own[
            pl.ds(pl.multiple_of(seat * block, block), block), :width
        ]


def vmem(count=1):
    return [pl.BlockSpec(memory_space=pltpu.VMEM)] * count


def smem(count=1):
    return [pl.BlockSpec(memory_space=pltpu.SMEM)] * count


def gather_blocks(own, size, order):
    blocks = {0: own}
    for i in sorted(range(1, size), key=lambda i: (bin(i).count("1"), -i)):
        low = i & -i
        blocks[i] = lax.ppermute(blocks[i ^ low], "tensor", xor_pairs(size, low))
    return jnp.concatenate([blocks[i] for i in order], axis=0)


def scatter_sum(rows, weight, size):
    half = rows.shape[0] // 2
    sent = jnp.dot(rows[:half], weight, preferred_element_type=jnp.float32).astype(jnp.bfloat16)
    arrived = lax.ppermute(sent, "tensor", xor_pairs(size, 1))
    total = jnp.dot(rows[half:], weight, preferred_element_type=jnp.float32)
    total = total + arrived.astype(jnp.float32)
    mask = 2
    while mask < size:
        half //= 2
        arrived = lax.ppermute(total[:half].astype(jnp.bfloat16), "tensor", xor_pairs(size, mask))
        total = total[half:] + arrived.astype(jnp.float32)
        mask *= 2
    return total


def attend_branch(
    caps, n_seq, n_tensor, table, normed, attn_query, attn_key, attn_value, buckets, weights, prefix_kv, groups, branch_of
):
    parts = spans(caps)
    hop_group = -(-(n_seq // 2) // STAGES)
    nodes = n_seq * prefix_kv.shape[1]
    width = prefix_kv.shape[3]
    order = block_order(n_tensor)
    sizes = [(high - low) * GRAIN for low, high, _ in parts]
    shapes = [jax.ShapeDtypeStruct((size, 2 * width), jnp.bfloat16) for size in sizes]
    packed = pl.pallas_call(
        functools.partial(pack_kernel, n_seq, nodes, parts),
        out_shape=shapes * 2,
        in_specs=smem() + vmem(),
        out_specs=vmem(2 * len(shapes)),
        compiler_params=pltpu.CompilerParams(vmem_limit_bytes=24 * MIB),
    )(table, prefix_kv)
    landed = []
    for way in range(2):
        pairs = ring_pairs(n_seq, 1 if way == 0 else -1)
        for number, (_, _, stage) in enumerate(parts):
            moving = packed[way * len(parts) + number]
            for _ in range(stage * hop_group):
                moving = lax.ppermute(moving, "seq", pairs)
                landed.append(moving)
    rows = gather_blocks(normed, n_tensor, order)
    proj = jnp.concatenate(
        [
            jnp.dot(rows, weight, preferred_element_type=jnp.float32).astype(jnp.bfloat16)
            for weight in (attn_query, attn_key, attn_value)
        ],
        axis=1,
    )
    n_rows = rows.shape[0]
    cap = prefix_kv.shape[2]
    return pl.pallas_call(
        functools.partial(attention_kernel, n_seq, n_tensor, order, parts, hop_group),
        out_shape=jax.ShapeDtypeStruct((n_rows, width), jnp.bfloat16),
        in_specs=smem(3) + vmem(4 + len(landed)),
        out_specs=vmem()[0],
        scratch_shapes=[
            pltpu.VMEM((n_rows, 3 * width), jnp.bfloat16),
            pltpu.VMEM((3, cap, 2 * width), jnp.bfloat16),
            pltpu.VMEM((4, width // HEAD, 2 * n_rows), jnp.float32),
        ],
        compiler_params=pltpu.CompilerParams(vmem_limit_bytes=48 * MIB),
    )(table, groups, branch_of, buckets, weights, proj, prefix_kv, *landed)


def per_device(
    hidden,
    attn_gain,
    attn_query,
    attn_key,
    attn_value,
    attn_out,
    ff_gain,
    ff_gate,
    ff_up,
    ff_down,
    final_gain,
    embedding,
    rel_weight,
    bucket_table,
    prefix_kv,
    node_lengths,
    group_branch,
    node_slot,
    request_group,
):
    n_seq = lax.axis_size("seq")
    n_tensor = lax.axis_size("tensor")
    tensor_index = lax.axis_index("tensor")
    own_rows, width = hidden.shape
    assert request_group.shape[0] == n_seq
    order = block_order(n_tensor)
    slots_here, cap = prefix_kv.shape[1:3]
    most = slots_here * cap
    classes = []
    for caps in CLASSES + ((most,) * STAGES,):
        caps = tuple(min(c, most) for c in caps)
        if caps not in classes:
            classes.append(caps)
    groups = request_group[None, :]
    branch_of = group_branch[None, :]
    table = pl.pallas_call(
        functools.partial(plan_kernel, n_seq, slots_here, cap, classes),
        out_shape=jax.ShapeDtypeStruct((8, 128), jnp.int32),
        in_specs=vmem(4),
        out_specs=vmem()[0],
    )(node_lengths[None, :], node_slot[None, :], branch_of, groups)
    normed = rms_scale(hidden, attn_gain).astype(jnp.bfloat16)
    attn = lax.switch(
        table[7, 0],
        [functools.partial(attend_branch, caps, n_seq, n_tensor) for caps in classes],
        table,
        normed,
        attn_query,
        attn_key,
        attn_value,
        bucket_table[::-1][None, :],
        jnp.transpose(rel_weight),
        prefix_kv,
        groups,
        branch_of,
    )
    attn_sum = scatter_sum(attn, attn_out, n_tensor)
    mid = (hidden.astype(jnp.float32) + attn_sum).astype(jnp.bfloat16)
    rows = gather_blocks(rms_scale(mid, ff_gain).astype(jnp.bfloat16), n_tensor, order)
    gate_part = jnp.dot(rows, ff_gate, preferred_element_type=jnp.float32)
    up_part = jnp.dot(rows, ff_up, preferred_element_type=jnp.float32)
    inner = (jax.nn.gelu(gate_part, approximate=True) * up_part).astype(jnp.bfloat16)
    ff_summed = scatter_sum(inner, ff_down, n_tensor)
    hidden_out = (mid.astype(jnp.float32) + ff_summed).astype(jnp.bfloat16)
    last = hidden_out[own_rows - 1 :]
    copies = [
        lax.ppermute(last, "tensor", [(n_tensor - 1, i)]) for i in range(n_tensor - 1)
    ]
    last = jnp.where(tensor_index == n_tensor - 1, last, sum(copies[1:], copies[0]))
    seq_index = lax.axis_index("seq")
    shifted = [last] + [
        lax.ppermute(last, "seq", [(i, (i + k) % n_seq) for i in range(n_seq)])
        for k in range(1, n_seq)
    ]
    stacked = jnp.concatenate(shifted, axis=0)
    from_row = lax.rem(seq_index - jnp.arange(n_seq) + n_seq, n_seq)
    last_rows = stacked[from_row].astype(jnp.float32)
    mean_square = jnp.mean(last_rows * last_rows, axis=1)
    last_rms = jnp.sqrt(mean_square)
    final_rows = (last_rows * lax.rsqrt(mean_square + 1e-06)[:, None] * final_gain).astype(
        jnp.bfloat16
    )
    embed_cols = embedding.shape[1]
    columns = lax.dynamic_slice_in_dim(final_rows, tensor_index * embed_cols, embed_cols, 1)
    logits = lax.dot_general(
        columns, embedding, (((1,), (1,)), ((), ())), preferred_element_type=jnp.float32
    )
    mask = 1
    while mask < n_tensor:
        sent = logits.astype(jnp.bfloat16)
        arrived = lax.ppermute(sent, "tensor", xor_pairs(n_tensor, mask))
        logits = sent.astype(jnp.float32) + arrived.astype(jnp.float32)
        mask *= 2
    top = jnp.max(logits, axis=1)
    tops = [top] + [
        lax.ppermute(top, "seq", [(i, (i + k) % n_seq) for i in range(n_seq)])
        for k in range(1, n_seq)
    ]
    top_logit = functools.reduce(jnp.maximum, tops)
    return (hidden_out, last_rms, top_logit)


def solution(mesh):
    return jax.shard_map(
        per_device,
        mesh=mesh,
        in_specs=(
            P(("seq", "tensor"), None),
            P(),
            P(None, "tensor"),
            P(None, "tensor"),
            P(None, "tensor"),
            P("tensor", None),
            P(),
            P(None, "tensor"),
            P(None, "tensor"),
            P("tensor", None),
            P(),
            P("seq", "tensor"),
            P(None, "tensor"),
            P(),
            P(None, "seq", None, "tensor"),
            P(),
            P(),
            P(),
            P(),
        ),
        out_specs=(P(("seq", "tensor"), None), P(), P()),
        check_vma=False,
    )
```

time: 478 us -> 201 us (0.42); the launches traced: 470 us -> 204 us
  local copies, waits for them, and re-layouts: 143 us -> 3.86 us
  waiting for transfers between devices: 170 us -> 95.3 us
  blocking collectives: 69.9 us -> 0 us
  starting transfers between devices: 0.2 us -> 59.1 us
  matrix products: 51.9 us -> 11.2 us
  between operations: 23.5 us -> 2.04 us
  loops' own time: 0 us -> 15.6 us
  Pallas kernels: 0 us -> 11.3 us
  other arithmetic: 11.9 us -> 5.12 us
    all_gather x3 -> x0, waiting for transfers between devices: 116 us -> none  [the longest x1 99.1 us: per_device(): piece_kv = lax.all_gather(prefix_kv, 'seq', axis=1, tiled=True)]
    ppermute x0 -> x49, waiting for transfers between devices: none -> 95.3 us  [the longest x20 53.6 us: attend_branch(): moving = lax.ppermute(moving, 'seq', pairs)]
    ppermute x0 -> x49, starting transfers between devices: none -> 59.1 us  [the longest x20 25.2 us: attend_branch(): moving = lax.ppermute(moving, 'seq', pairs)]
    reduce_scatter x2 -> x0, waiting for transfers between devices: 54 us -> none  [the longest x1 29.7 us: per_device(): lax.psum_scatter(jnp.dot(attn, attn_out, preferred_element_type=jnp.float...]
    slice x19 -> x4, local copies, waits for them, and re-layouts: 47.2 us -> 0.59 us  [the longest x1 0.51 us: per_device(): table[7, 0]]
    all_gather x1 -> x0, blocking collectives: 41.3 us -> none  [per_device(): every_last = lax.all_gather(picked, ('seq', 'tensor'), axis=0, tiled=True)]
    dot_general x16 -> x9, matrix products: 48.6 us -> 7.89 us  [the longest x3 2.1 us: attend_branch(): jnp.dot(rows, weight, preferred_element_type=jnp.float32)]
    broadcast_in_dim x8 -> x0, local copies, waits for them, and re-layouts: 37.3 us -> none  [shifted_block(): jnp.broadcast_to(bias_slab[:, None, :], (heads_here, query_count, slab_len))]
  transfers between devices with their start and end apart: 5 -> 49, of which waited for: 4 -> 24; matrix products, arithmetic and copies ran while one was open for 30% -> 2% of each run, Pallas kernels for 0% -> 0%
where the time goes in v1:
time: 201 us; the launch traced here: 204 us
  waiting for transfers between devices  95.3 us (47%)
  starting transfers between devices  59.1 us (29%)
  loops' own time  15.6 us (8%)
  Pallas kernels  11.3 us (6%)
  matrix products  11.2 us (6%)
  other arithmetic  5.12 us (3%)
  local copies, waits for them, and re-layouts  3.86 us (2%)
  between operations  2.04 us (1%)
    ppermute x20, waiting for transfers between devices, attend_branch(): moving = lax.ppermute(moving, 'seq', pairs)  53.6 us
    ppermute x20, starting transfers between devices, attend_branch(): moving = lax.ppermute(moving, 'seq', pairs)  25.2 us
    another operation x1, loops' own time, per_device(): lax.switch(table[7, 0], [functools.partial(attend_branch, caps, n_seq, n_...  15.6 us
    ppermute x2, waiting for transfers between devices, scatter_sum(): lax.ppermute(total[:half].astype(jnp.bfloat16), 'tensor', xor_pairs(size,...  13.7 us
    ppermute x6, waiting for transfers between devices, gather_blocks(): blocks[i] = lax.ppermute(blocks[i ^ low], 'tensor', xor_pairs(size, low))  13.6 us
    ppermute x7, starting transfers between devices, per_device(): lax.ppermute(last, 'seq', [(i, (i + k) % n_seq) for i in range(n_seq)])  12.5 us
    ppermute x7, starting transfers between devices, per_device(): lax.ppermute(top, 'seq', [(i, (i + k) % n_seq) for i in range(n_seq)])  9.72 us
    pallas_call x1, Pallas kernels, attend_branch(): pl.pallas_call(functools.partial(attention_kernel, n_seq, n_tensor, order...  7.65 us
  transfers between devices with their start and end apart: 49, of which 24 were waited for; matrix products, arithmetic and copies ran while one was open for 2% of the time, Pallas kernels for 0%

profile of v1, /device:TPU:0, one launch (start us, length us, event | category | flops | bytes accessed | tf_op | source)
XLA Modules:
  0.0 203.6 jit_solution(13246406938096731)
XLA Ops:
  0.6 1.3 fusion.9
  1.9 0.8 rev.3
  2.7 1.1 shard_map.226
  4.3 1.1 fusion.11
  6.0 116.5 %conditional.1 = (bf16[256,512]{1,0:T(8,128)(2,1)S(1)}) conditional(s32[]{:T(128)} %bitcast.10, (bf16[64,2048]{1,0:T(8,128)(2,1)S(1)}, bf16[2048,512]{1,0:T(8,128)(2,1)}, bf16[2048,512]{1,0:T(8,128)(2,1)}, bf16[2048,512]{1,0:T(8,128)(2,1)}, s32[8,128]{1,0:T(8,128)S(1)}, /*index=5*/bf16[2,4,256,512]{3,2,1,0:T(8,128)(2,1)}, ...), branch_computations={%region_1.0_spmd, %region_2.0_spmd, %region_3.0_spmd, %region_4.0_... | conditional | flops 1613365248 | bytes 168039712 | solution.py:418
  14.9 2.6 %branch_4_fun.2 = (bf16[352,1024]{1,0:T(8,128)(2,1)S(1)}, bf16[48,1024]{1,0:T(8,128)(2,1)S(1)}, bf16[112,1024]{1,0:T(8,128)(2,1)S(1)}, bf16[64,1024]{1,0:T(8,128...) custom-call(s32[8,128]{1,0:T(8,128)S(1)} %get-tuple-element.199.tabl, ...), custom_call_target="tpu_custom_call" | custom-call | tf_op jit(solution)/shard_map/cond/branch_4_fun/pallas_call | solution.py:336
  17.5 3.1 %collective-permute-start.105 = (bf16[352,1024]{1,0:T(8,128)(2,1)S(1)}, bf16[352,1024]{1,0:T(8,128)(2,1)S(1)}, u32[]{:S(2)}, u32[]{:S(2)}) collective-permute-start(bf16[352,1024]{1,0:T(8,128)(2,1)S(1)} %get-tuple-element.213), channel_id=1, source_target_pairs={{0,4},{8,0},{16,8},{24,16},{28,24},{20,28},{12,20},{4,12},{1,5},{9... | collective-permute-start | bytes 2162696 | tf_op jit(solution)/shard_map/cond/branch_4_fun/ppermute | solution.py:349
  20.8 1.7 collective-permute-start.92
  22.5 6.1 %collective-permute-done.92 = bf16[64,2048]{1,0:T(8,128)(2,1)S(1)} collective-permute-done((bf16[64,2048]{1,0:T(8,128)(2,1)S(1)}, bf16[64,2048]{1,0:T(8,128)(2,1)S(1)}, u32[]{:S(2)}, u32[]{:S(2)}) %collective-permute-start.92) | collective-permute-done | bytes 262176 | tf_op jit(solution)/shard_map/cond/branch_4_fun/ppermute | solution.py:307
  28.6 8.3 %collective-permute-done.105.rest_10_ = bf16[352,1024]{1,0:T(8,128)(2,1)S(1)} collective-permute-done((bf16[352,1024]{1,0:T(8,128)(2,1)S(1)}, bf16[352,1024]{1,0:T(8,128)(2,1)S(1)}, u32[]{:S(2)}, u32[]{:S(2)}) %collective-permute-start.105) | collective-permute-done | bytes 720928 | tf_op jit(solution)/shard_map/cond/branch_4_fun/ppermute | solution.py:349
  36.9 1.6 collective-permute-start.106
  38.9 1.7 collective-permute-start.99
  41.0 1.8 collective-permute-start.104
  42.8 12.5 %collective-permute-done.106.rest_11_ = bf16[352,1024]{1,0:T(8,128)(2,1)S(1)} collective-permute-done((bf16[352,1024]{1,0:T(8,128)(2,1)S(1)}, bf16[352,1024]{1,0:T(8,128)(2,1)S(1)}, u32[]{:S(2)}, u32[]{:S(2)}) %collective-permute-start.106) | collective-permute-done | bytes 720928 | tf_op jit(solution)/shard_map/cond/branch_4_fun/ppermute | solution.py:349
  55.3 1.6 collective-permute-start.107
  58.1 0.7 convolution_convert_fusion.12
  58.8 0.9 collective-permute-done.99.rest_4_
  59.7 1.7 collective-permute-start.114
  61.7 0.8 collective-permute-done.104.rest_9_
  62.5 1.9 collective-permute-start.110
  64.4 10.0 %collective-permute-done.107.rest_12_ = bf16[352,1024]{1,0:T(8,128)(2,1)S(1)} collective-permute-done((bf16[352,1024]{1,0:T(8,128)(2,1)S(1)}, bf16[352,1024]{1,0:T(8,128)(2,1)S(1)}, u32[]{:S(2)}, u32[]{:S(2)}) %collective-permute-start.107) | collective-permute-done | bytes 720928 | tf_op jit(solution)/shard_map/cond/branch_4_fun/ppermute | solution.py:349
  74.4 1.6 collective-permute-start.108
  76.0 1.3 collective-permute-done.97.rest_2_
  78.4 1.8 collective-permute-start.102
  80.2 0.9 collective-permute-start.112
  81.1 1.1 collective-permute-start.101
  83.0 16.1 %collective-permute-done.102.rest_7_ = bf16[112,1024]{1,0:T(8,128)(2,1)S(1)} collective-permute-done((bf16[112,1024]{1,0:T(8,128)(2,1)S(1)}, bf16[112,1024]{1,0:T(8,128)(2,1)S(1)}, u32[]{:S(2)}, u32[]{:S(2)}) %collective-permute-start.102) | collective-permute-done | bytes 229408 | tf_op jit(solution)/shard_map/cond/branch_4_fun/ppermute | solution.py:349
  99.1 2.1 %collective-permute-start.111 = (bf16[48,1024]{1,0:T(8,128)(2,1)S(1)}, bf16[48,1024]{1,0:T(8,128)(2,1)S(1)}, u32[]{:S(2)}, u32[]{:S(2)}) collective-permute-start(bf16[48,1024]{1,0:T(8,128)(2,1)S(1)} %collective-permute-done.110.rest_15_), channel_id=1, source_target_pairs={{0,4},{8,0},{16,8},{24,16},{28,24},{20,28},{12,20},{4,12},{1,5},{9... | collective-permute-start | bytes 294920 | tf_op jit(solution)/shard_map/cond/branch_4_fun/ppermute | solution.py:349
  101.3 2.1 %collective-permute-start.113 = (bf16[112,1024]{1,0:T(8,128)(2,1)S(1)}, bf16[112,1024]{1,0:T(8,128)(2,1)S(1)}, u32[]{:S(2)}, u32[]{:S(2)}) collective-permute-start(bf16[112,1024]{1,0:T(8,128)(2,1)S(1)} %collective-permute-done.112.rest_17_), channel_id=1, source_target_pairs={{0,4},{8,0},{16,8},{24,16},{28,24},{20,28},{12,20},{4,12},{1,5},{9... | collective-permute-start | bytes 688136 | tf_op jit(solution)/shard_map/cond/branch_4_fun/ppermute | solution.py:349
  103.3 0.9 pad_maximum_fusion.4.proj
  104.3 3.0 %collective-permute-done.103.rest_8_ = bf16[112,1024]{1,0:T(8,128)(2,1)S(1)} collective-permute-done((bf16[112,1024]{1,0:T(8,128)(2,1)S(1)}, bf16[112,1024]{1,0:T(8,128)(2,1)S(1)}, u32[]{:S(2)}, u32[]{:S(2)}) %collective-permute-start.103) | collective-permute-done | bytes 229408 | tf_op jit(solution)/shard_map/cond/branch_4_fun/ppermute | solution.py:349
  107.3 0.9 copy-done.15
  108.2 7.6 %branch_4_fun.3 = bf16[256,512]{1,0:T(8,128)(2,1)S(1)} custom-call(s32[8,128]{1,0:T(8,128)S(1)} %get-tuple-element.199.table, s32[1,8]{1,0:T(1,128)S(1)} %copy-done.33, s32[1,24]{1,0:T(1,128)S(1)} %copy-done.27, s32[1,2048]{1,0:T(1,128)S(1)} %bitcast.63, f32[8,32]{1,0:T(8,128)S(1)} %copy-done.21, bf16[256,1536]{1,0:T(8,128)(2,1)} %pad_maximum_fusion.4.proj, ...), custom_call_target="tpu_custom_call" | custom-call | tf_op jit(solution)/shard_map/cond/branch_4_fun/pallas_call | solution.py:361
  123.1 1.9 collective-permute-done.126
  125.5 1.6 collective-permute-start.127
  127.1 6.8 %collective-permute-done.127 = bf16[64,2048]{1,0:T(8,128)(2,1)S(1)} collective-permute-done((bf16[64,2048]{1,0:T(8,128)(2,1)S(1)}, bf16[64,2048]{1,0:T(8,128)(2,1)S(1)}, u32[]{:S(2)}, u32[]{:S(2)}) %collective-permute-start.127) | collective-permute-done | bytes 262176 | tf_op jit(solution)/shard_map/ppermute | solution.py:320
  134.3 1.6 collective-permute-start.128
  135.9 6.0 %collective-permute-done.128 = bf16[64,2048]{1,0:T(8,128)(2,1)S(1)} collective-permute-done((bf16[64,2048]{1,0:T(8,128)(2,1)S(1)}, bf16[64,2048]{1,0:T(8,128)(2,1)S(1)}, u32[]{:S(2)}, u32[]{:S(2)}) %collective-permute-start.128) | collective-permute-done | bytes 262176 | tf_op jit(solution)/shard_map/ppermute | solution.py:307
  141.9 1.5 collective-permute-done.129
  143.5 1.5 fusion.23
  145.0 1.6 fusion.8
  146.6 0.9 convolution_convert_fusion.19
  147.7 1.8 collective-permute-done.131
  149.5 0.9 convert_add_fusion
  150.4 1.6 collective-permute-start.132
  152.0 6.9 %collective-permute-done.132 = bf16[64,2048]{1,0:T(8,128)(2,1)S(1)} collective-permute-done((bf16[64,2048]{1,0:T(8,128)(2,1)S(1)}, bf16[64,2048]{1,0:T(8,128)(2,1)S(1)}, u32[]{:S(2)}, u32[]{:S(2)}) %collective-permute-start.132) | collective-permute-done | bytes 262176 | tf_op jit(solution)/shard_map/ppermute | solution.py:320
  159.0 1.3 collective-permute-start.133
  161.6 2.3 %collective-permute-done.133 = bf16[1,2048]{1,0:T(2,128)(2,1)S(1)} collective-permute-done((bf16[1,2048]{1,0:T(2,128)(2,1)S(1)}, bf16[1,2048]{1,0:T(2,128)(2,1)S(1)}, u32[]{:S(2)}, u32[]{:S(2)}) %collective-permute-start.133) | collective-permute-done | bytes 4128 | tf_op jit(solution)/shard_map/ppermute | solution.py:442
  164.0 2.0 collective-permute-start.136
  166.0 1.8 collective-permute-start.137
  167.8 2.2 %collective-permute-start.138 = (bf16[1,2048]{1,0:T(2,128)(2,1)S(1)}, bf16[1,2048]{1,0:T(2,128)(2,1)S(1)}, u32[]{:S(2)}, u32[]{:S(2)}) collective-permute-start(bf16[1,2048]{1,0:T(2,128)(2,1)S(1)} %broadcast_select_fusion), channel_id=1, source_target_pairs={{0,12},{4,16},{8,20},{12,24},{16,28},{20,0},{24,4},{28,8},{1,13},{... | collective-permute-start | bytes 12296 | tf_op jit(solution)/shard_map/ppermute | solution.py:447
  170.4 3.0 %collective-permute-start.140 = (bf16[1,2048]{1,0:T(2,128)(2,1)S(1)}, bf16[1,2048]{1,0:T(2,128)(2,1)S(1)}, u32[]{:S(2)}, u32[]{:S(2)}) collective-permute-start(bf16[1,2048]{1,0:T(2,128)(2,1)S(1)} %broadcast_select_fusion), channel_id=1, source_target_pairs={{0,20},{4,24},{8,28},{12,0},{16,4},{20,8},{24,12},{28,16},{1,21},{... | collective-permute-start | bytes 12296 | tf_op jit(solution)/shard_map/ppermute | solution.py:447
  173.4 2.8 %collective-permute-start.141 = (bf16[1,2048]{1,0:T(2,128)(2,1)S(1)}, bf16[1,2048]{1,0:T(2,128)(2,1)S(1)}, u32[]{:S(2)}, u32[]{:S(2)}) collective-permute-start(bf16[1,2048]{1,0:T(2,128)(2,1)S(1)} %broadcast_select_fusion), channel_id=1, source_target_pairs={{0,24},{4,28},{8,0},{12,4},{16,8},{20,12},{24,16},{28,20},{1,25},{... | collective-permute-start | bytes 12296 | tf_op jit(solution)/shard_map/ppermute | solution.py:447
  176.5 0.8 dynamic-slice
  177.6 2.3 %collective-permute-done.142 = bf16[1,2048]{1,0:T(2,128)(2,1)S(1)} collective-permute-done((bf16[1,2048]{1,0:T(2,128)(2,1)S(1)}, bf16[1,2048]{1,0:T(2,128)(2,1)S(1)}, u32[]{:S(2)}, u32[]{:S(2)}) %collective-permute-start.142) | collective-permute-done | bytes 4128 | tf_op jit(solution)/shard_map/ppermute | solution.py:447
  181.2 3.3 %convolution_convert_fusion.18 = bf16[8,4016]{1,0:T(8,128)(2,1)S(1)} fusion(bf16[4016,512]{1,0:T(8,128)(2,1)} %param.36, f32[8,2048]{1,0:T(8,128)S(1)} %convert_element_type.134, s32[]{:T(128)S(6)} %select_n.24, f32[512]{0:T(512)S(1)} %dynamic-slice, f32[8]{0:T(128)S(1)} %get-tuple-element.288), kind=kOutput, calls=%fused_computation.49 | convolution fusion | flops 32943488 | bytes 4195588 | tf_op jit(solution)/shard_map/dot_general | solution.py:460
  184.6 1.3 collective-permute-done.143
  185.9 2.4 %collective-permute-start.144 = (bf16[8,4016]{1,0:T(8,128)(2,1)S(1)}, bf16[8,4016]{1,0:T(8,128)(2,1)S(1)}, u32[]{:S(2)}, u32[]{:S(2)}) collective-permute-start(bf16[8,4016]{1,0:T(8,128)(2,1)S(1)} %add_convert_fusion), channel_id=1, source_target_pairs={{0,2},{1,3},{2,0},{3,1},{4,6},{5,7},{6,4},{7,5},{8,10},{9,11},{10,... | collective-permute-start | bytes 192776 | tf_op jit(solution)/shard_map/ppermute | solution.py:466
  188.2 2.4 %collective-permute-done.144 = bf16[8,4016]{1,0:T(8,128)(2,1)S(1)} collective-permute-done((bf16[8,4016]{1,0:T(8,128)(2,1)S(1)}, bf16[8,4016]{1,0:T(8,128)(2,1)S(1)}, u32[]{:S(2)}, u32[]{:S(2)}) %collective-permute-start.144) | collective-permute-done | bytes 64288 | tf_op jit(solution)/shard_map/ppermute | solution.py:466
  191.5 3.2 %collective-permute-start.147 = (f32[8]{0:T(128)S(1)}, f32[8]{0:T(128)S(1)}, u32[]{:S(2)}, u32[]{:S(2)}) collective-permute-start(f32[8]{0:T(128)S(1)} %add_reduce_fusion), channel_id=1, source_target_pairs={{0,12},{4,16},{8,20},{12,24},{16,28},{20,0},{24,4},{28,8},{1,13},{... | collective-permute-start | bytes 104 | tf_op jit(solution)/shard_map/ppermute | solution.py:471
  194.7 1.5 collective-permute-start.148
  196.1 2.6 %collective-permute-start.149 = (f32[8]{0:T(128)S(1)}, f32[8]{0:T(128)S(1)}, u32[]{:S(2)}, u32[]{:S(2)}) collective-permute-start(f32[8]{0:T(128)S(1)} %add_reduce_fusion), channel_id=1, source_target_pairs={{0,20},{4,24},{8,28},{12,0},{16,4},{20,8},{24,12},{28,16},{1,21},{... | collective-permute-start | bytes 104 | tf_op jit(solution)/shard_map/ppermute | solution.py:471
  199.1 1.5 collective-permute-start.151
  200.6 1.7 collective-permute-done.150
  (115 shorter events, 12.5 us)
Async XLA Ops:
  0.6 121.9 %copy-start = (bf16[512,2048]{1,0:T(8,128)(2,1)S(1)}, bf16[512,2048]{1,0:T(8,128)(2,1)}, u32[]{:S(2)}) copy-start(bf16[512,2048]{1,0:T(8,128)(2,1)} %param.30) | copy-start | bytes 6291460
  14.9 43.2 %copy-start.53 = (bf16[2048,512]{1,0:T(8,128)(2,1)S(1)}, bf16[2048,512]{1,0:T(8,128)(2,1)}, u32[]{:S(2)}) copy-start(bf16[2048,512]{1,0:T(8,128)(2,1)} %get-tuple-element.278) | copy-start | bytes 6291460 | tf_op jit(solution)/shard_map/cond
  17.5 19.4 %collective-permute-start.105 = (bf16[352,1024]{1,0:T(8,128)(2,1)S(1)}, bf16[352,1024]{1,0:T(8,128)(2,1)S(1)}, u32[]{:S(2)}, u32[]{:S(2)}) collective-permute-start(bf16[352,1024]{1,0:T(8,128)(2,1)S(1)} %get-tuple-element.213), channel_id=1, source_target_pairs={{0,4},{8,0},{16,8},{24,16},{28,24},{20,28},{12,20},{4,12},{1,5},{9... | collective-permute-start | bytes 2162696 | tf_op jit(solution)/shard_map/cond/branch_4_fun/ppermute | solution.py:349
  20.6 17.9 %collective-permute-start.95 = (bf16[352,1024]{1,0:T(8,128)(2,1)S(1)}, bf16[352,1024]{1,0:T(8,128)(2,1)S(1)}, u32[]{:S(2)}, u32[]{:S(2)}) collective-permute-start(bf16[352,1024]{1,0:T(8,128)(2,1)S(1)} %get-tuple-element.209), channel_id=1, source_target_pairs={{0,8},{8,16},{16,24},{24,28},{28,20},{20,12},{12,4},{4,0},{1,9},{9... | collective-permute-start | bytes 2162696 | tf_op jit(solution)/shard_map/cond/branch_4_fun/ppermute | solution.py:349
  20.8 7.8 %collective-permute-start.92 = (bf16[64,2048]{1,0:T(8,128)(2,1)S(1)}, bf16[64,2048]{1,0:T(8,128)(2,1)S(1)}, u32[]{:S(2)}, u32[]{:S(2)}) collective-permute-start(bf16[64,2048]{1,0:T(8,128)(2,1)S(1)} %get-tuple-element.204), channel_id=1, source_target_pairs={{0,2},{1,3},{2,0},{3,1},{4,6},{5,7},{6,4},{7,5},{8,10},{9,11},{10,... | collective-permute-start | bytes 786440 | tf_op jit(solution)/shard_map/cond/branch_4_fun/ppermute | solution.py:307
  28.6 12.1 %collective-permute-start.93 = (bf16[64,2048]{1,0:T(8,128)(2,1)S(1)}, bf16[64,2048]{1,0:T(8,128)(2,1)S(1)}, u32[]{:S(2)}, u32[]{:S(2)}) collective-permute-start(bf16[64,2048]{1,0:T(8,128)(2,1)S(1)} %collective-permute-done.92), channel_id=1, source_target_pairs={{0,1},{1,0},{2,3},{3,2},{4,5},{5,4},{6,7},{7,6},{8,9},{9,8},{10,11... | collective-permute-start | bytes 786440 | tf_op jit(solution)/shard_map/cond/branch_4_fun/ppermute | solution.py:307
  36.9 18.4 %collective-permute-start.106 = (bf16[352,1024]{1,0:T(8,128)(2,1)S(1)}, bf16[352,1024]{1,0:T(8,128)(2,1)S(1)}, u32[]{:S(2)}, u32[]{:S(2)}) collective-permute-start(bf16[352,1024]{1,0:T(8,128)(2,1)S(1)} %collective-permute-done.105.rest_10_), channel_id=1, source_target_pairs={{0,4},{8,0},{16,8},{24,16},{28,24},{20,28},{12,20},{4,12},{1,5},{9... | collective-permute-start | bytes 2162696 | tf_op jit(solution)/shard_map/cond/branch_4_fun/ppermute | solution.py:349
  38.5 19.1 %collective-permute-start.96 = (bf16[352,1024]{1,0:T(8,128)(2,1)S(1)}, bf16[352,1024]{1,0:T(8,128)(2,1)S(1)}, u32[]{:S(2)}, u32[]{:S(2)}) collective-permute-start(bf16[352,1024]{1,0:T(8,128)(2,1)S(1)} %collective-permute-done.95.rest_0_), channel_id=1, source_target_pairs={{0,8},{8,16},{16,24},{24,28},{28,20},{20,12},{12,4},{4,0},{1,9},{9... | collective-permute-start | bytes 2162696 | tf_op jit(solution)/shard_map/cond/branch_4_fun/ppermute | solution.py:349
  38.9 2.1 %collective-permute-start.94 = (bf16[64,2048]{1,0:T(8,128)(2,1)S(1)}, bf16[64,2048]{1,0:T(8,128)(2,1)S(1)}, u32[]{:S(2)}, u32[]{:S(2)}) collective-permute-start(bf16[64,2048]{1,0:T(8,128)(2,1)S(1)} %get-tuple-element.204), channel_id=1, source_target_pairs={{0,1},{1,0},{2,3},{3,2},{4,5},{5,4},{6,7},{7,6},{8,9},{9,8},{10,11... | collective-permute-start | bytes 786440 | tf_op jit(solution)/shard_map/cond/branch_4_fun/ppermute | solution.py:307
  38.9 20.7 %collective-permute-start.99 = (bf16[48,1024]{1,0:T(8,128)(2,1)S(1)}, bf16[48,1024]{1,0:T(8,128)(2,1)S(1)}, u32[]{:S(2)}, u32[]{:S(2)}) collective-permute-start(bf16[48,1024]{1,0:T(8,128)(2,1)S(1)} %get-tuple-element.210), channel_id=1, source_target_pairs={{0,8},{8,16},{16,24},{24,28},{28,20},{20,12},{12,4},{4,0},{1,9},{9... | collective-permute-start | bytes 294920 | tf_op jit(solution)/shard_map/cond/branch_4_fun/ppermute | solution.py:349
  40.7 20.7 %collective-permute-start.109 = (bf16[48,1024]{1,0:T(8,128)(2,1)S(1)}, bf16[48,1024]{1,0:T(8,128)(2,1)S(1)}, u32[]{:S(2)}, u32[]{:S(2)}) collective-permute-start(bf16[48,1024]{1,0:T(8,128)(2,1)S(1)} %get-tuple-element.214), channel_id=1, source_target_pairs={{0,4},{8,0},{16,8},{24,16},{28,24},{20,28},{12,20},{4,12},{1,5},{9... | collective-permute-start | bytes 294920 | tf_op jit(solution)/shard_map/cond/branch_4_fun/ppermute | solution.py:349
  41.0 21.5 %collective-permute-start.104 = (bf16[64,1024]{1,0:T(8,128)(2,1)S(1)}, bf16[64,1024]{1,0:T(8,128)(2,1)S(1)}, u32[]{:S(2)}, u32[]{:S(2)}) collective-permute-start(bf16[64,1024]{1,0:T(8,128)(2,1)S(1)} %get-tuple-element.212), channel_id=1, source_target_pairs={{0,8},{8,16},{16,24},{24,28},{28,20},{20,12},{12,4},{4,0},{1,9},{9... | collective-permute-start | bytes 393224 | tf_op jit(solution)/shard_map/cond/branch_4_fun/ppermute | solution.py:349
  55.3 19.1 %collective-permute-start.107 = (bf16[352,1024]{1,0:T(8,128)(2,1)S(1)}, bf16[352,1024]{1,0:T(8,128)(2,1)S(1)}, u32[]{:S(2)}, u32[]{:S(2)}) collective-permute-start(bf16[352,1024]{1,0:T(8,128)(2,1)S(1)} %collective-permute-done.106.rest_11_), channel_id=1, source_target_pairs={{0,4},{8,0},{16,8},{24,16},{28,24},{20,28},{12,20},{4,12},{1,5},{9... | collective-permute-start | bytes 2162696 | tf_op jit(solution)/shard_map/cond/branch_4_fun/ppermute | solution.py:349
  57.6 19.7 %collective-permute-start.97 = (bf16[352,1024]{1,0:T(8,128)(2,1)S(1)}, bf16[352,1024]{1,0:T(8,128)(2,1)S(1)}, u32[]{:S(2)}, u32[]{:S(2)}) collective-permute-start(bf16[352,1024]{1,0:T(8,128)(2,1)S(1)} %collective-permute-done.96.rest_1_), channel_id=1, source_target_pairs={{0,8},{8,16},{16,24},{24,28},{28,20},{20,12},{12,4},{4,0},{1,9},{9... | collective-permute-start | bytes 2162696 | tf_op jit(solution)/shard_map/cond/branch_4_fun/ppermute | solution.py:349
  58.0 19.7 %copy-start.47 = (bf16[2048,512]{1,0:T(8,128)(2,1)S(1)}, bf16[2048,512]{1,0:T(8,128)(2,1)}, u32[]{:S(2)}) copy-start(bf16[2048,512]{1,0:T(8,128)(2,1)} %get-tuple-element.272) | copy-start | bytes 6291460 | tf_op jit(solution)/shard_map/cond
  58.8 23.5 %copy-start.41 = (bf16[2048,512]{1,0:T(8,128)(2,1)S(1)}, bf16[2048,512]{1,0:T(8,128)(2,1)}, u32[]{:S(2)}) copy-start(bf16[2048,512]{1,0:T(8,128)(2,1)} %get-tuple-element.266) | copy-start | bytes 6291460 | tf_op jit(solution)/shard_map/cond
  59.7 18.7 %collective-permute-start.114 = (bf16[64,1024]{1,0:T(8,128)(2,1)S(1)}, bf16[64,1024]{1,0:T(8,128)(2,1)S(1)}, u32[]{:S(2)}, u32[]{:S(2)}) collective-permute-start(bf16[64,1024]{1,0:T(8,128)(2,1)S(1)} %get-tuple-element.216), channel_id=1, source_target_pairs={{0,4},{8,0},{16,8},{24,16},{28,24},{20,28},{12,20},{4,12},{1,5},{9... | collective-permute-start | bytes 393224 | tf_op jit(solution)/shard_map/cond/branch_4_fun/ppermute | solution.py:349
  61.4 18.8 %collective-permute-start.100 = (bf16[48,1024]{1,0:T(8,128)(2,1)S(1)}, bf16[48,1024]{1,0:T(8,128)(2,1)S(1)}, u32[]{:S(2)}, u32[]{:S(2)}) collective-permute-start(bf16[48,1024]{1,0:T(8,128)(2,1)S(1)} %collective-permute-done.99.rest_4_), channel_id=1, source_target_pairs={{0,8},{8,16},{16,24},{24,28},{28,20},{20,12},{12,4},{4,0},{1,9},{9... | collective-permute-start | bytes 294920 | tf_op jit(solution)/shard_map/cond/branch_4_fun/ppermute | solution.py:349
  62.5 18.6 %collective-permute-start.110 = (bf16[48,1024]{1,0:T(8,128)(2,1)S(1)}, bf16[48,1024]{1,0:T(8,128)(2,1)S(1)}, u32[]{:S(2)}, u32[]{:S(2)}) collective-permute-start(bf16[48,1024]{1,0:T(8,128)(2,1)S(1)} %collective-permute-done.109.rest_14_), channel_id=1, source_target_pairs={{0,4},{8,0},{16,8},{24,16},{28,24},{20,28},{12,20},{4,12},{1,5},{9... | collective-permute-start | bytes 294920 | tf_op jit(solution)/shard_map/cond/branch_4_fun/ppermute | solution.py:349
  74.4 8.6 %copy-start.14 = (bf16[352,1024]{1,0:T(8,128)(2,1)}, bf16[352,1024]{1,0:T(8,128)(2,1)S(1)}, u32[]{:S(2)}) copy-start(bf16[352,1024]{1,0:T(8,128)(2,1)S(1)} %collective-permute-done.107.rest_12_) | copy-start | bytes 2162692 | tf_op jit(solution)/shard_map/cond
  74.4 33.0 %collective-permute-start.108 = (bf16[352,1024]{1,0:T(8,128)(2,1)S(1)}, bf16[352,1024]{1,0:T(8,128)(2,1)S(1)}, u32[]{:S(2)}, u32[]{:S(2)}) collective-permute-start(bf16[352,1024]{1,0:T(8,128)(2,1)S(1)} %collective-permute-done.107.rest_12_), channel_id=1, source_target_pairs={{0,4},{8,0},{16,8},{24,16},{28,24},{20,28},{12,20},{4,12},{1,5},{9... | collective-permute-start | bytes 2162696 | tf_op jit(solution)/shard_map/cond/branch_4_fun/ppermute | solution.py:349
  77.3 30.1 %collective-permute-start.98 = (bf16[352,1024]{1,0:T(8,128)(2,1)S(1)}, bf16[352,1024]{1,0:T(8,128)(2,1)S(1)}, u32[]{:S(2)}, u32[]{:S(2)}) collective-permute-start(bf16[352,1024]{1,0:T(8,128)(2,1)S(1)} %collective-permute-done.97.rest_2_), channel_id=1, source_target_pairs={{0,8},{8,16},{16,24},{24,28},{28,20},{20,12},{12,4},{4,0},{1,9},{9... | collective-permute-start | bytes 2162696 | tf_op jit(solution)/shard_map/cond/branch_4_fun/ppermute | solution.py:349
  78.4 20.7 %collective-permute-start.102 = (bf16[112,1024]{1,0:T(8,128)(2,1)S(1)}, bf16[112,1024]{1,0:T(8,128)(2,1)S(1)}, u32[]{:S(2)}, u32[]{:S(2)}) collective-permute-start(bf16[112,1024]{1,0:T(8,128)(2,1)S(1)} %get-tuple-element.211), channel_id=1, source_target_pairs={{0,8},{8,16},{16,24},{24,28},{28,20},{20,12},{12,4},{4,0},{1,9},{9... | collective-permute-start | bytes 688136 | tf_op jit(solution)/shard_map/cond/branch_4_fun/ppermute | solution.py:349
  80.2 21.0 %collective-permute-start.112 = (bf16[112,1024]{1,0:T(8,128)(2,1)S(1)}, bf16[112,1024]{1,0:T(8,128)(2,1)S(1)}, u32[]{:S(2)}, u32[]{:S(2)}) collective-permute-start(bf16[112,1024]{1,0:T(8,128)(2,1)S(1)} %get-tuple-element.215), channel_id=1, source_target_pairs={{0,4},{8,0},{16,8},{24,16},{28,24},{20,28},{12,20},{4,12},{1,5},{9... | collective-permute-start | bytes 688136 | tf_op jit(solution)/shard_map/cond/branch_4_fun/ppermute | solution.py:349
  81.1 20.1 %collective-permute-start.101 = (bf16[48,1024]{1,0:T(8,128)(2,1)S(1)}, bf16[48,1024]{1,0:T(8,128)(2,1)S(1)}, u32[]{:S(2)}, u32[]{:S(2)}) collective-permute-start(bf16[48,1024]{1,0:T(8,128)(2,1)S(1)} %collective-permute-done.100.rest_5_), channel_id=1, source_target_pairs={{0,8},{8,16},{16,24},{24,28},{28,20},{20,12},{12,4},{4,0},{1,9},{9... | collective-permute-start | bytes 294920 | tf_op jit(solution)/shard_map/cond/branch_4_fun/ppermute | solution.py:349
  82.2 26.0 %copy-start.5 = (bf16[2,4,256,512]{3,2,1,0:T(8,128)(2,1)S(1)}, bf16[2,4,256,512]{3,2,1,0:T(8,128)(2,1)}, u32[]{:S(2)}) copy-start(bf16[2,4,256,512]{3,2,1,0:T(8,128)(2,1)} %get-tuple-element.284.cache) | copy-start | bytes 6291460 | tf_op jit(solution)/shard_map/cond
  82.2 26.0 %copy-start.21 = (f32[8,32]{1,0:T(8,128)S(1)}, f32[8,32]{1,0:T(8,128)}, u32[]{:S(2)}) copy-start(f32[8,32]{1,0:T(8,128)} %get-tuple-element.203.weights) | copy-start | bytes 3076 | tf_op jit(solution)/shard_map/cond
  82.2 26.0 %copy-start.27 = (s32[1,24]{1,0:T(1,128)S(1)}, s32[1,24]{1,0:T(1,128)}, u32[]{:S(2)}) copy-start(s32[1,24]{1,0:T(1,128)} %get-tuple-element.201.branch_of) | copy-start | bytes 292 | tf_op jit(solution)/shard_map/cond
  82.2 26.0 %copy-start.33 = (s32[1,8]{1,0:T(1,128)S(1)}, s32[1,8]{1,0:T(1,128)}, u32[]{:S(2)}) copy-start(s32[1,8]{1,0:T(1,128)} %get-tuple-element.200.groups) | copy-start | bytes 100 | tf_op jit(solution)/shard_map/cond
  99.1 5.2 %collective-permute-start.111 = (bf16[48,1024]{1,0:T(8,128)(2,1)S(1)}, bf16[48,1024]{1,0:T(8,128)(2,1)S(1)}, u32[]{:S(2)}, u32[]{:S(2)}) collective-permute-start(bf16[48,1024]{1,0:T(8,128)(2,1)S(1)} %collective-permute-done.110.rest_15_), channel_id=1, source_target_pairs={{0,4},{8,0},{16,8},{24,16},{28,24},{20,28},{12,20},{4,12},{1,5},{9... | collective-permute-start | bytes 294920 | tf_op jit(solution)/shard_map/cond/branch_4_fun/ppermute | solution.py:349
  101.2 6.0 %collective-permute-start.103 = (bf16[112,1024]{1,0:T(8,128)(2,1)S(1)}, bf16[112,1024]{1,0:T(8,128)(2,1)S(1)}, u32[]{:S(2)}, u32[]{:S(2)}) collective-permute-start(bf16[112,1024]{1,0:T(8,128)(2,1)S(1)} %collective-permute-done.102.rest_7_), channel_id=1, source_target_pairs={{0,8},{8,16},{16,24},{24,28},{28,20},{20,12},{12,4},{4,0},{1,9},{9... | collective-permute-start | bytes 688136 | tf_op jit(solution)/shard_map/cond/branch_4_fun/ppermute | solution.py:349
  101.3 6.1 %collective-permute-start.113 = (bf16[112,1024]{1,0:T(8,128)(2,1)S(1)}, bf16[112,1024]{1,0:T(8,128)(2,1)S(1)}, u32[]{:S(2)}, u32[]{:S(2)}) collective-permute-start(bf16[112,1024]{1,0:T(8,128)(2,1)S(1)} %collective-permute-done.112.rest_17_), channel_id=1, source_target_pairs={{0,4},{8,0},{16,8},{24,16},{28,24},{20,28},{12,20},{4,12},{1,5},{9... | collective-permute-start | bytes 688136 | tf_op jit(solution)/shard_map/cond/branch_4_fun/ppermute | solution.py:349
  123.0 10.9 %copy-start.7 = (bf16[64,2048]{1,0:T(8,128)(2,1)S(1)}, bf16[64,2048]{1,0:T(8,128)(2,1)}, u32[]{:S(2)}) copy-start(bf16[64,2048]{1,0:T(8,128)(2,1)} %param.25) | copy-start | bytes 786436
  123.0 11.2 %copy-start.35 = (f32[2048]{0:T(1024)S(1)}, f32[2048]{0:T(1024)}, u32[]{:S(2)}) copy-start(f32[2048]{0:T(1024)} %param.31) | copy-start | bytes 24580
  123.0 2.0 collective-permute-start.126
  125.0 18.5 %copy-start.36 = (bf16[2048,1280]{1,0:T(8,128)(2,1)S(1)}, bf16[2048,1280]{1,0:T(8,128)(2,1)}, u32[]{:S(2)}) copy-start(bf16[2048,1280]{1,0:T(8,128)(2,1)} %param.32) | copy-start | bytes 15728644
  125.5 8.4 %collective-permute-start.127 = (bf16[64,2048]{1,0:T(8,128)(2,1)S(1)}, bf16[64,2048]{1,0:T(8,128)(2,1)S(1)}, u32[]{:S(2)}, u32[]{:S(2)}) collective-permute-start(bf16[64,2048]{1,0:T(8,128)(2,1)S(1)} %slice.75), channel_id=1, source_target_pairs={{0,2},{1,3},{2,0},{3,1},{4,6},{5,7},{6,4},{7,5},{8,10},{9,11},{10,... | collective-permute-start | bytes 786440 | tf_op jit(solution)/shard_map/ppermute | solution.py:320
  134.2 10.8 %slice-start.2 = ((s8[5242880]{0:T(1024)(128)(4,1)}), s8[4194304]{0:T(1024)(128)(4,1)S(1)}, s32[]{:S(2)}) async-start(s8[5242880]{0:T(1024)(128)(4,1)} %bitcast.87), calls=%async_computation.2 | async-start | bytes 8388608
  134.3 10.7 %slice-start.3 = ((s8[5242880]{0:T(1024)(128)(4,1)}), s8[1048576]{0:T(1024)(128)(4,1)S(1)}, s32[]{:S(2)}) async-start(s8[5242880]{0:T(1024)(128)(4,1)} %bitcast.87), calls=%async_computation.3 | async-start | bytes 2097152
  134.3 7.6 %collective-permute-start.128 = (bf16[64,2048]{1,0:T(8,128)(2,1)S(1)}, bf16[64,2048]{1,0:T(8,128)(2,1)S(1)}, u32[]{:S(2)}, u32[]{:S(2)}) collective-permute-start(bf16[64,2048]{1,0:T(8,128)(2,1)S(1)} %fusion.15), channel_id=1, source_target_pairs={{0,2},{1,3},{2,0},{3,1},{4,6},{5,7},{6,4},{7,5},{8,10},{9,11},{10,... | collective-permute-start | bytes 786440 | tf_op jit(solution)/shard_map/ppermute | solution.py:307
  135.9 6.0 %collective-permute-start.130 = (bf16[64,2048]{1,0:T(8,128)(2,1)S(1)}, bf16[64,2048]{1,0:T(8,128)(2,1)S(1)}, u32[]{:S(2)}, u32[]{:S(2)}) collective-permute-start(bf16[64,2048]{1,0:T(8,128)(2,1)S(1)} %fusion.15), channel_id=1, source_target_pairs={{0,1},{1,0},{2,3},{3,2},{4,5},{5,4},{6,7},{7,6},{8,9},{9,8},{10,11... | collective-permute-start | bytes 786440 | tf_op jit(solution)/shard_map/ppermute | solution.py:307
  141.9 1.5 collective-permute-start.129
  147.5 2.0 collective-permute-start.131
  150.4 8.4 %collective-permute-start.132 = (bf16[64,2048]{1,0:T(8,128)(2,1)S(1)}, bf16[64,2048]{1,0:T(8,128)(2,1)S(1)}, u32[]{:S(2)}, u32[]{:S(2)}) collective-permute-start(bf16[64,2048]{1,0:T(8,128)(2,1)S(1)} %slice.74), channel_id=1, source_target_pairs={{0,2},{1,3},{2,0},{3,1},{4,6},{5,7},{6,4},{7,5},{8,10},{9,11},{10,... | collective-permute-start | bytes 786440 | tf_op jit(solution)/shard_map/ppermute | solution.py:320
  158.9 25.6 %copy-start.16 = (bf16[64,2048]{1,0:T(8,128)(2,1)}, bf16[64,2048]{1,0:T(8,128)(2,1)S(1)}, u32[]{:S(2)}) copy-start(bf16[64,2048]{1,0:T(8,128)(2,1)S(1)} %fusion.16) | copy-start | bytes 786436
  159.0 5.0 %collective-permute-start.133 = (bf16[1,2048]{1,0:T(2,128)(2,1)S(1)}, bf16[1,2048]{1,0:T(2,128)(2,1)S(1)}, u32[]{:S(2)}, u32[]{:S(2)}) collective-permute-start(bf16[1,2048]{1,0:T(2,128)(2,1)S(1)} %slice.52), channel_id=1, source_target_pairs={{3,0},{7,4},{11,8},{15,12},{19,16},{23,20},{27,24},{31,28}} | collective-permute-start | bytes 12296 | tf_op jit(solution)/shard_map/ppermute | solution.py:442
  160.3 3.7 %collective-permute-start.134 = (bf16[1,2048]{1,0:T(2,128)(2,1)S(1)}, bf16[1,2048]{1,0:T(2,128)(2,1)S(1)}, u32[]{:S(2)}, u32[]{:S(2)}) collective-permute-start(bf16[1,2048]{1,0:T(2,128)(2,1)S(1)} %slice.52), channel_id=1, source_target_pairs={{3,1},{7,5},{11,9},{15,13},{19,17},{23,21},{27,25},{31,29}} | collective-permute-start | bytes 12296 | tf_op jit(solution)/shard_map/ppermute | solution.py:442
  160.9 3.0 %collective-permute-start.135 = (bf16[1,2048]{1,0:T(2,128)(2,1)S(1)}, bf16[1,2048]{1,0:T(2,128)(2,1)S(1)}, u32[]{:S(2)}, u32[]{:S(2)}) collective-permute-start(bf16[1,2048]{1,0:T(2,128)(2,1)S(1)} %slice.52), channel_id=1, source_target_pairs={{3,2},{7,6},{11,10},{15,14},{19,18},{23,22},{27,26},{31,30}} | collective-permute-start | bytes 12296 | tf_op jit(solution)/shard_map/ppermute | solution.py:442
  164.0 9.5 %collective-permute-start.136 = (bf16[1,2048]{1,0:T(2,128)(2,1)S(1)}, bf16[1,2048]{1,0:T(2,128)(2,1)S(1)}, u32[]{:S(2)}, u32[]{:S(2)}) collective-permute-start(bf16[1,2048]{1,0:T(2,128)(2,1)S(1)} %broadcast_select_fusion), channel_id=1, source_target_pairs={{0,4},{4,8},{8,12},{12,16},{16,20},{20,24},{24,28},{28,0},{1,5},{5... | collective-permute-start | bytes 12296 | tf_op jit(solution)/shard_map/ppermute | solution.py:447
  166.0 10.2 %collective-permute-start.137 = (bf16[1,2048]{1,0:T(2,128)(2,1)S(1)}, bf16[1,2048]{1,0:T(2,128)(2,1)S(1)}, u32[]{:S(2)}, u32[]{:S(2)}) collective-permute-start(bf16[1,2048]{1,0:T(2,128)(2,1)S(1)} %broadcast_select_fusion), channel_id=1, source_target_pairs={{0,8},{4,12},{8,16},{12,20},{16,24},{20,28},{24,0},{28,4},{1,9},{5... | collective-permute-start | bytes 12296 | tf_op jit(solution)/shard_map/ppermute | solution.py:447
  167.8 9.5 %collective-permute-start.138 = (bf16[1,2048]{1,0:T(2,128)(2,1)S(1)}, bf16[1,2048]{1,0:T(2,128)(2,1)S(1)}, u32[]{:S(2)}, u32[]{:S(2)}) collective-permute-start(bf16[1,2048]{1,0:T(2,128)(2,1)S(1)} %broadcast_select_fusion), channel_id=1, source_target_pairs={{0,12},{4,16},{8,20},{12,24},{16,28},{20,0},{24,4},{28,8},{1,13},{... | collective-permute-start | bytes 12296 | tf_op jit(solution)/shard_map/ppermute | solution.py:447
  170.0 7.3 %collective-permute-start.139 = (bf16[1,2048]{1,0:T(2,128)(2,1)S(1)}, bf16[1,2048]{1,0:T(2,128)(2,1)S(1)}, u32[]{:S(2)}, u32[]{:S(2)}) collective-permute-start(bf16[1,2048]{1,0:T(2,128)(2,1)S(1)} %broadcast_select_fusion), channel_id=1, source_target_pairs={{0,16},{4,20},{8,24},{12,28},{16,0},{20,4},{24,8},{28,12},{1,17},{... | collective-permute-start | bytes 12296 | tf_op jit(solution)/shard_map/ppermute | solution.py:447
  170.4 6.8 %collective-permute-start.140 = (bf16[1,2048]{1,0:T(2,128)(2,1)S(1)}, bf16[1,2048]{1,0:T(2,128)(2,1)S(1)}, u32[]{:S(2)}, u32[]{:S(2)}) collective-permute-start(bf16[1,2048]{1,0:T(2,128)(2,1)S(1)} %broadcast_select_fusion), channel_id=1, source_target_pairs={{0,20},{4,24},{8,28},{12,0},{16,4},{20,8},{24,12},{28,16},{1,21},{... | collective-permute-start | bytes 12296 | tf_op jit(solution)/shard_map/ppermute | solution.py:447
  173.4 4.1 %collective-permute-start.141 = (bf16[1,2048]{1,0:T(2,128)(2,1)S(1)}, bf16[1,2048]{1,0:T(2,128)(2,1)S(1)}, u32[]{:S(2)}, u32[]{:S(2)}) collective-permute-start(bf16[1,2048]{1,0:T(2,128)(2,1)S(1)} %broadcast_select_fusion), channel_id=1, source_target_pairs={{0,24},{4,28},{8,0},{12,4},{16,8},{20,12},{24,16},{28,20},{1,25},{... | collective-permute-start | bytes 12296 | tf_op jit(solution)/shard_map/ppermute | solution.py:447
  176.2 3.7 %collective-permute-start.142 = (bf16[1,2048]{1,0:T(2,128)(2,1)S(1)}, bf16[1,2048]{1,0:T(2,128)(2,1)S(1)}, u32[]{:S(2)}, u32[]{:S(2)}) collective-permute-start(bf16[1,2048]{1,0:T(2,128)(2,1)S(1)} %broadcast_select_fusion), channel_id=1, source_target_pairs={{0,28},{4,0},{8,4},{12,8},{16,12},{20,16},{24,20},{28,24},{1,29},{... | collective-permute-start | bytes 12296 | tf_op jit(solution)/shard_map/ppermute | solution.py:447
  184.6 1.3 collective-permute-start.143
  185.9 4.8 %collective-permute-start.144 = (bf16[8,4016]{1,0:T(8,128)(2,1)S(1)}, bf16[8,4016]{1,0:T(8,128)(2,1)S(1)}, u32[]{:S(2)}, u32[]{:S(2)}) collective-permute-start(bf16[8,4016]{1,0:T(8,128)(2,1)S(1)} %add_convert_fusion), channel_id=1, source_target_pairs={{0,2},{1,3},{2,0},{3,1},{4,6},{5,7},{6,4},{7,5},{8,10},{9,11},{10,... | collective-permute-start | bytes 192776 | tf_op jit(solution)/shard_map/ppermute | solution.py:466
  190.8 8.0 %collective-permute-start.145 = (f32[8]{0:T(128)S(1)}, f32[8]{0:T(128)S(1)}, u32[]{:S(2)}, u32[]{:S(2)}) collective-permute-start(f32[8]{0:T(128)S(1)} %add_reduce_fusion), channel_id=1, source_target_pairs={{0,4},{4,8},{8,12},{12,16},{16,20},{20,24},{24,28},{28,0},{1,5},{5... | collective-permute-start | bytes 104 | tf_op jit(solution)/shard_map/ppermute | solution.py:471
  191.4 7.7 %collective-permute-start.146 = (f32[8]{0:T(128)S(1)}, f32[8]{0:T(128)S(1)}, u32[]{:S(2)}, u32[]{:S(2)}) collective-permute-start(f32[8]{0:T(128)S(1)} %add_reduce_fusion), channel_id=1, source_target_pairs={{0,8},{4,12},{8,16},{12,20},{16,24},{20,28},{24,0},{28,4},{1,9},{5... | collective-permute-start | bytes 104 | tf_op jit(solution)/shard_map/ppermute | solution.py:471
  191.5 9.0 %collective-permute-start.147 = (f32[8]{0:T(128)S(1)}, f32[8]{0:T(128)S(1)}, u32[]{:S(2)}, u32[]{:S(2)}) collective-permute-start(f32[8]{0:T(128)S(1)} %add_reduce_fusion), channel_id=1, source_target_pairs={{0,12},{4,16},{8,20},{12,24},{16,28},{20,0},{24,4},{28,8},{1,13},{... | collective-permute-start | bytes 104 | tf_op jit(solution)/shard_map/ppermute | solution.py:471
  194.7 5.9 %collective-permute-start.148 = (f32[8]{0:T(128)S(1)}, f32[8]{0:T(128)S(1)}, u32[]{:S(2)}, u32[]{:S(2)}) collective-permute-start(f32[8]{0:T(128)S(1)} %add_reduce_fusion), channel_id=1, source_target_pairs={{0,16},{4,20},{8,24},{12,28},{16,0},{20,4},{24,8},{28,12},{1,17},{... | collective-permute-start | bytes 104 | tf_op jit(solution)/shard_map/ppermute | solution.py:471
  196.1 4.4 %collective-permute-start.149 = (f32[8]{0:T(128)S(1)}, f32[8]{0:T(128)S(1)}, u32[]{:S(2)}, u32[]{:S(2)}) collective-permute-start(f32[8]{0:T(128)S(1)} %add_reduce_fusion), channel_id=1, source_target_pairs={{0,20},{4,24},{8,28},{12,0},{16,4},{20,8},{24,12},{28,16},{1,21},{... | collective-permute-start | bytes 104 | tf_op jit(solution)/shard_map/ppermute | solution.py:471
  198.8 3.5 %collective-permute-start.150 = (f32[8]{0:T(128)S(1)}, f32[8]{0:T(128)S(1)}, u32[]{:S(2)}, u32[]{:S(2)}) collective-permute-start(f32[8]{0:T(128)S(1)} %add_reduce_fusion), channel_id=1, source_target_pairs={{0,24},{4,28},{8,0},{12,4},{16,8},{20,12},{24,16},{28,20},{1,25},{... | collective-permute-start | bytes 104 | tf_op jit(solution)/shard_map/ppermute | solution.py:471
  199.1 3.5 %collective-permute-start.151 = (f32[8]{0:T(128)S(1)}, f32[8]{0:T(128)S(1)}, u32[]{:S(2)}, u32[]{:S(2)}) collective-permute-start(f32[8]{0:T(128)S(1)} %add_reduce_fusion), channel_id=1, source_target_pairs={{0,28},{4,0},{8,4},{12,8},{16,12},{20,16},{24,20},{28,24},{1,29},{... | collective-permute-start | bytes 104 | tf_op jit(solution)/shard_map/ppermute | solution.py:471
  (3 other events, 5.7 us)
